TPU v7x, 256 devices: a whole 4x4x8 slice. The times are simulated.
256 devices in a mesh: frame: 32 (over z, y_hi, core), patch: 8 (over x, y_lo).
Axes of the slice: x: 4, y: 4 (y_hi: 2, y_lo: 2; y = y_hi * 2 + y_lo), z: 8, core: 2. Of those that a mesh axis runs over, the one named last changes fastest.
Arguments:
- stream: bfloat16 [64, 880, 1024], P('frame', 'patch'), may hold values from -6 to 6
- spatial_out: bfloat16 [64, 880, 512], P('frame', 'patch'), may hold values from -6 to 6
- spatial_qkv: bfloat16 [64, 880, 1536], P('frame', 'patch'), may hold values from -6 to 6
- upstream: bfloat16 [64, 880, 1024], P('frame', 'patch'), may hold values from -6 to 6
- proj_spatial: bfloat16 [512, 1024], replicated, may hold values from -0.25 to 0.25
- qkv_temporal: bfloat16 [1024, 3072], replicated, may hold values from -0.75 to 0.75
- proj_temporal: bfloat16 [1024, 1024], replicated, may hold values from -0.1875 to 0.1875
- mod_weight: bfloat16 [256, 1024], replicated, may hold values from -0.25 to 0.25
- noise_steps: int32 [64], P('frame'), may hold values from 0 to 999
- positions: int32 [64], replicated, may hold values from 0 to 63, each once
- memory: int32 [64, 4], replicated, may hold values from 0 to 63
Outputs:
- grad_stream: bfloat16 [64, 880, 1024], P('frame', 'patch')
- grad_spatial_qkv: bfloat16 [64, 880, 1536], P('frame', 'patch')
- grad_proj_spatial: float32 [512, 1024], P('frame', 'patch')
- grad_qkv_temporal: float32 [1024, 3072], P('frame', 'patch')
- grad_proj_temporal: float32 [1024, 1024], P('frame', 'patch')
All inputs are finite; a program needn't handle non-finite values.
Results may differ from a plain program's by a relative error of at most 0.027.
Values may be sent and summed in bfloat16 or wider, within the bound.
A program may use at most 128 MiB of HBM per device.

v0:
```python
import jax
import jax.numpy as jnp
from jax import lax
from jax.sharding import PartitionSpec as P

H = 16


def frame_embedding(noise_steps, embed_width):
    half_width = embed_width // 2
    counter = jnp.arange(half_width, dtype=jnp.float32)
    frequency = jnp.exp(-jnp.log(10000.0) * counter / half_width)
    angles = noise_steps.astype(jnp.float32)[:, None] * frequency[None, :]
    return jnp.concatenate([jnp.cos(angles), jnp.sin(angles)], axis=1)


def visible_frames(positions, memory):
    frame_total = positions.shape[0]
    earlier = positions[None, :] <= positions[:, None]
    frame_ids = jnp.arange(frame_total, dtype=jnp.int32)
    recalled = jnp.any(memory[:, :, None] == frame_ids[None, None, :], axis=1)
    return jnp.logical_or(earlier, recalled)


def attend_grad(
    query_matrix_rows, key_matrix_rows, value_matrix_rows, gradient_rows, allowed, logit_scale
):
    logit_scores = (
        jnp.einsum(
            "hud,hzd->huz", query_matrix_rows, key_matrix_rows, preferred_element_type=jnp.float32
        )
        * logit_scale
    )
    if allowed is not None:
        logit_scores = jnp.where(allowed, logit_scores, -1e30)
    row_max = jnp.max(logit_scores, axis=-1, keepdims=True)
    lifted = jnp.exp(logit_scores - row_max)
    attn_probs = lifted / jnp.sum(lifted, axis=-1, keepdims=True)
    probability_narrow = attn_probs.astype(jnp.bfloat16)
    final_answer = jnp.einsum(
        "rtl,rlp->rtp", probability_narrow, value_matrix_rows, preferred_element_type=jnp.float32
    ).astype(jnp.bfloat16)
    probability_gradient = jnp.einsum(
        "hud,hzd->huz", gradient_rows, value_matrix_rows, preferred_element_type=jnp.float32
    )
    center = jnp.sum(attn_probs * probability_gradient, axis=-1, keepdims=True)
    score_gradient = (attn_probs * (probability_gradient - center) * logit_scale).astype(
        jnp.bfloat16
    )
    query_gradient = jnp.einsum(
        "rtl,rlp->rtp", score_gradient, key_matrix_rows, preferred_element_type=jnp.float32
    ).astype(jnp.bfloat16)
    key_gradient = jnp.einsum(
        "pfd,pfn->pdn", score_gradient, query_matrix_rows, preferred_element_type=jnp.float32
    ).astype(jnp.bfloat16)
    value_gradient = jnp.einsum(
        "pfd,pfn->pdn", probability_narrow, gradient_rows, preferred_element_type=jnp.float32
    ).astype(jnp.bfloat16)
    return (final_answer, query_gradient, key_gradient, value_gradient)


def shards(
    stream,
    spatial_out,
    spatial_qkv,
    upstream,
    proj_spatial,
    qkv_temporal,
    proj_temporal,
    mod_weight,
    noise_steps,
    positions,
    memory,
):
    local_frames, local_tokens, model_width = stream.shape
    head_count = H
    head_width = model_width // head_count
    logit_scale = head_width ** (-0.5)
    frame_devices = lax.axis_size("frame")
    patch_devices = lax.axis_size("patch")
    token_count = local_frames * local_tokens
    embedding = frame_embedding(noise_steps, mod_weight.shape[0]).astype(jnp.bfloat16)
    frame_gain = 1.0 + jnp.dot(embedding, mod_weight, preferred_element_type=jnp.float32)
    stream_wide = stream.astype(jnp.float32)
    inverse = lax.rsqrt(jnp.mean(stream_wide * stream_wide, axis=-1, keepdims=True) + 1e-06)
    normed = (stream_wide * inverse * frame_gain[:, None, :]).astype(jnp.bfloat16)
    normed_rows = normed.reshape(token_count, model_width)
    upstream_rows = upstream.reshape(token_count, model_width)
    projected = jnp.dot(normed_rows, qkv_temporal, preferred_element_type=jnp.float32).astype(
        jnp.bfloat16
    )
    projected = projected.reshape(local_frames, local_tokens, 3, head_count, head_width)
    grad_out_t = jnp.dot(upstream_rows, proj_temporal.T, preferred_element_type=jnp.float32).astype(
        jnp.bfloat16
    )
    grad_out_t = grad_out_t.reshape(local_frames, local_tokens, head_count, head_width)
    pair_group = local_tokens * head_count // frame_devices
    frame_total = local_frames * frame_devices

    def to_pairs(tensor):
        return tensor.reshape(local_frames, frame_devices, pair_group, head_width)

    arrived = (
        lax.all_to_all(
            to_pairs(projected[:, :, 0]), "frame", split_axis=1, concat_axis=0, tiled=True
        ),
        lax.all_to_all(
            to_pairs(projected[:, :, 1]), "frame", split_axis=1, concat_axis=0, tiled=True
        ),
        lax.all_to_all(
            to_pairs(projected[:, :, 2]), "frame", split_axis=1, concat_axis=0, tiled=True
        ),
        lax.all_to_all(to_pairs(grad_out_t), "frame", split_axis=1, concat_axis=0, tiled=True),
    )
    allowed = visible_frames(positions, memory)

    def pair_major(tensor):
        return jnp.transpose(tensor.reshape(frame_total, pair_group, head_width), (1, 0, 2))

    def frame_major(tensor):
        return jnp.transpose(tensor, (1, 0, 2)).reshape(frame_total, 1, pair_group, head_width)

    outcome = attend_grad(
        pair_major(arrived[0]),
        pair_major(arrived[1]),
        pair_major(arrived[2]),
        pair_major(arrived[3]),
        allowed,
        logit_scale,
    )
    returned = (
        lax.all_to_all(frame_major(outcome[0]), "frame", split_axis=0, concat_axis=1, tiled=True),
        lax.all_to_all(frame_major(outcome[1]), "frame", split_axis=0, concat_axis=1, tiled=True),
        lax.all_to_all(frame_major(outcome[2]), "frame", split_axis=0, concat_axis=1, tiled=True),
        lax.all_to_all(frame_major(outcome[3]), "frame", split_axis=0, concat_axis=1, tiled=True),
    )

    def token_heads(tensor):
        return tensor.reshape(local_frames, local_tokens, head_count, head_width)

    temporal_o = returned[0].reshape(token_count, model_width)
    grad_qkv_rows = jnp.stack(
        [token_heads(returned[1]), token_heads(returned[2]), token_heads(returned[3])], axis=2
    ).reshape(token_count, 3 * model_width)
    term_proj_temporal = jnp.dot(temporal_o.T, upstream_rows, preferred_element_type=jnp.float32)
    term_qkv_temporal = jnp.dot(normed_rows.T, grad_qkv_rows, preferred_element_type=jnp.float32)
    grad_normed = jnp.dot(
        grad_qkv_rows, qkv_temporal.T, preferred_element_type=jnp.float32
    ).reshape(local_frames, local_tokens, model_width)
    scaled = grad_normed * frame_gain[:, None, :]
    inner_mean = jnp.mean(stream_wide * scaled, axis=-1, keepdims=True)
    grad_stream = (
        upstream.astype(jnp.float32) + inverse * scaled - stream_wide * inverse**3 * inner_mean
    ).astype(jnp.bfloat16)
    stream_rows = grad_stream.reshape(token_count, model_width)
    spatial_heads = spatial_out.shape[2] // head_width
    heads_here = spatial_heads // patch_devices
    frame_tokens = local_tokens * patch_devices
    grad_out_s = jnp.dot(stream_rows, proj_spatial.T, preferred_element_type=jnp.float32).astype(
        jnp.bfloat16
    )
    grad_out_s = grad_out_s.reshape(local_frames, local_tokens, spatial_heads, head_width)
    term_proj_spatial = jnp.dot(
        spatial_out.reshape(token_count, spatial_heads * head_width).T,
        stream_rows,
        preferred_element_type=jnp.float32,
    )
    split_qkv = spatial_qkv.reshape(local_frames, local_tokens, 3, spatial_heads, head_width)
    gathered = (
        lax.all_to_all(split_qkv[:, :, 0], "patch", split_axis=2, concat_axis=1, tiled=True),
        lax.all_to_all(split_qkv[:, :, 1], "patch", split_axis=2, concat_axis=1, tiled=True),
        lax.all_to_all(split_qkv[:, :, 2], "patch", split_axis=2, concat_axis=1, tiled=True),
        lax.all_to_all(grad_out_s, "patch", split_axis=2, concat_axis=1, tiled=True),
    )

    def head_major(tensor):
        return jnp.transpose(tensor, (0, 2, 1, 3)).reshape(
            local_frames * heads_here, frame_tokens, head_width
        )

    def token_major(tensor):
        return jnp.transpose(
            tensor.reshape(local_frames, heads_here, frame_tokens, head_width), (0, 2, 1, 3)
        )

    spatial = attend_grad(
        head_major(gathered[0]),
        head_major(gathered[1]),
        head_major(gathered[2]),
        head_major(gathered[3]),
        None,
        logit_scale,
    )
    sent_back = (
        lax.all_to_all(token_major(spatial[1]), "patch", split_axis=1, concat_axis=2, tiled=True),
        lax.all_to_all(token_major(spatial[2]), "patch", split_axis=1, concat_axis=2, tiled=True),
        lax.all_to_all(token_major(spatial[3]), "patch", split_axis=1, concat_axis=2, tiled=True),
    )
    grad_spatial_qkv = jnp.stack([sent_back[0], sent_back[1], sent_back[2]], axis=2).reshape(
        local_frames, local_tokens, 3 * spatial_heads * head_width
    )
    sectioned = (
        lax.psum_scatter(
            term_proj_spatial.astype(jnp.bfloat16), "frame", scatter_dimension=0, tiled=True
        ).astype(jnp.float32),
        lax.psum_scatter(
            term_qkv_temporal.astype(jnp.bfloat16), "frame", scatter_dimension=0, tiled=True
        ).astype(jnp.float32),
        lax.psum_scatter(
            term_proj_temporal.astype(jnp.bfloat16), "frame", scatter_dimension=0, tiled=True
        ).astype(jnp.float32),
    )
    summed = (
        lax.psum_scatter(
            sectioned[0].astype(jnp.bfloat16), "patch", scatter_dimension=1, tiled=True
        ).astype(jnp.float32),
        lax.psum_scatter(
            sectioned[1].astype(jnp.bfloat16), "patch", scatter_dimension=1, tiled=True
        ).astype(jnp.float32),
        lax.psum_scatter(
            sectioned[2].astype(jnp.bfloat16), "patch", scatter_dimension=1, tiled=True
        ).astype(jnp.float32),
    )
    return (grad_stream, grad_spatial_qkv, summed[0], summed[1], summed[2])


def solution(mesh):
    in_specs = (
        P("frame", "patch", None),
        P("frame", "patch", None),
        P("frame", "patch", None),
        P("frame", "patch", None),
        P(),
        P(),
        P(),
        P(),
        P("frame"),
        P(),
        P(),
    )
    out_specs = (
        P("frame", "patch", None),
        P("frame", "patch", None),
        P("frame", "patch"),
        P("frame", "patch"),
        P("frame", "patch"),
    )
    return jax.shard_map(shards, mesh=mesh, in_specs=in_specs, out_specs=out_specs, check_vma=False)
```

profile of v0, /device:TPU:16, one launch (start us, length us, event | category | flops | bytes accessed | tf_op | source)
XLA Modules:
  0.0 707.9 jit_solution(16541438480173566956)
XLA Ops:
  12.9 11.6 %all-to-all-start.2 = ((bf16[32,2,3520]{2,1,0:T(2,128)(2,1)}), bf16[32,2,3520]{2,1,0:T(2,128)(2,1)}, u32[]{:S(2)}, u32[]{:S(2)}) async-start(bf16[32,2,3520]{2,1,0:T(2,128)(2,1)} %reshape.141), calls=%async_computation.2 | async-start | bytes 917504 | tf_op jit(solution)/shard_map/all_to_all | solution.py:113
  25.4 5.6 convolution_convert_fusion.1
  31.0 1.7 copy.127
  33.6 2.1 fusion.104
  38.1 2.8 all-to-all-done.2
  40.9 7.0 all-to-all-start
  50.2 14.0 %all-to-all-done = bf16[32,2,3520]{2,1,0:T(2,128)(2,1)S(1)} async-done(((bf16[32,2,3520]{2,1,0:T(2,128)(2,1)}), bf16[32,2,3520]{2,1,0:T(2,128)(2,1)S(1)}, u32[]{:S(2)}, u32[]{:S(2)}) %all-to-all-start) | async-done | bytes 450592 | tf_op jit(solution)/shard_map/all_to_all | solution.py:104
  64.2 5.0 all-to-all-start.3
  71.6 13.9 %all-to-all-done.3 = bf16[32,2,3520]{2,1,0:T(2,128)(2,1)S(1)} async-done(((bf16[32,2,3520]{2,1,0:T(2,128)(2,1)}), bf16[32,2,3520]{2,1,0:T(2,128)(2,1)S(1)}, u32[]{:S(2)}, u32[]{:S(2)}) %all-to-all-start.3) | async-done | bytes 450592 | tf_op jit(solution)/shard_map/all_to_all | solution.py:110
  85.5 5.3 all-to-all-start.1
  91.0 2.8 reshape.142
  96.8 1.9 copy.130
  101.2 5.8 all-to-all-done.1
  109.4 1.8 fusion.107
  111.2 3.2 fusion.105
  114.5 3.8 fusion.43
  120.2 5.5 all-to-all-start.5
  125.7 1.9 fusion.41
  129.5 12.3 %all-to-all-done.5 = bf16[32,2,3520]{2,1,0:T(2,128)(2,1)S(1)} async-done(((bf16[32,2,3520]{2,1,0:T(2,128)(2,1)}), bf16[32,2,3520]{2,1,0:T(2,128)(2,1)S(1)}, u32[]{:S(2)}, u32[]{:S(2)}) %all-to-all-start.5) | async-done | bytes 450592 | tf_op jit(solution)/shard_map/all_to_all | solution.py:134
  141.9 5.0 all-to-all-start.6
  146.9 4.9 fusion.46
  151.8 1.8 copy.141
  154.9 8.3 %all-to-all-done.6 = bf16[32,2,3520]{2,1,0:T(2,128)(2,1)S(1)} async-done(((bf16[32,2,3520]{2,1,0:T(2,128)(2,1)}), bf16[32,2,3520]{2,1,0:T(2,128)(2,1)S(1)}, u32[]{:S(2)}, u32[]{:S(2)}) %all-to-all-start.6) | async-done | bytes 450592 | tf_op jit(solution)/shard_map/all_to_all | solution.py:135
  163.2 5.0 all-to-all-start.4
  172.5 12.0 %all-to-all-done.4 = bf16[32,2,3520]{2,1,0:T(2,128)(2,1)S(1)} async-done(((bf16[32,2,3520]{2,1,0:T(2,128)(2,1)}), bf16[32,2,3520]{2,1,0:T(2,128)(2,1)S(1)}, u32[]{:S(2)}, u32[]{:S(2)}) %all-to-all-start.4) | async-done | bytes 450592 | tf_op jit(solution)/shard_map/all_to_all | solution.py:133
  189.7 3.4 copy.147
  193.1 5.4 fusion.73
  200.9 2.3 copy.184
  203.2 2.2 fusion.42
  206.9 2.8 reshape.159
  209.7 21.4 %all_to_all.225 = bf16[32,2,3520]{2,1,0:T(2,128)(2,1)} all-to-all(bf16[32,2,3520]{2,1,0:T(2,128)(2,1)} %reshape.159), channel_id=1, replica_groups=mesh['frame'=32,'patch'=8] {'frame'}, dimensions={0} | all-to-all | bytes 901120 | tf_op jit(solution)/shard_map/all_to_all | solution.py:132
  231.1 3.0 reshape.160
  234.1 2.2 copy.205
  236.3 2.6 reshape.130
  239.0 3.2 convolution_convert_fusion.2
  242.2 3.9 copy.168
  246.1 2.7 reshape.128
  248.9 4.5 convolution_convert_fusion
  256.1 5.0 all-to-all-start.8
  261.8 6.2 all-to-all-done.8
  268.1 3.4 all-to-all-start.7
  272.6 5.7 all-to-all-done.7
  278.3 3.4 all-to-all-start.10
  283.8 4.8 all-to-all-done.10
  288.6 3.4 all-to-all-start.9
  292.1 4.7 fusion.106
  297.2 1.8 all-to-all-done.9
  299.3 3.6 fusion.108
  303.0 10.7 %reduce-scatter.19.cloned.1.call-done = bf16[16,1024]{1,0:T(8,128)(2,1)} async-done(((bf16[512,1024]{1,0:T(8,128)(2,1)}), bf16[16,1024]{1,0:T(8,128)(2,1)}) %reduce-scatter.19.cloned.1.call-update) | async-done | bytes 32784
  315.3 10.1 %fusion.61 = bf16[2,880,1,64]{1,3,0,2:T(8,128)(2,1)S(1)} fusion(bf16[2,880,64]{1,2,0:T(8,128)(2,1)S(1)} %copy-done.19, f32[2,880,880]{1,2,0:T(8,128)} %fusion.108, f32[2,880,880]{1,2,0:T(8,128)} %get-tuple-element.40, f32[2,880]{1,0:T(2,128)S(1)} %get-tuple-element.39), kind=kOutput, calls=%fused_computation.50 | convolution fusion | flops 209203280 | bytes 12848000 | tf_op jit(solution)/shard_map/pfd,pfn->pdn/dot_general | solution.py:53
  327.1 4.9 all-to-all-start.12
  332.0 103.7 %reduce-scatter.17.cloned.1.call-done = bf16[32,1024]{1,0:T(8,128)(2,1)} async-done(((bf16[1024,1024]{1,0:T(8,128)(2,1)}), bf16[32,1024]{1,0:T(8,128)(2,1)}) %reduce-scatter.17.cloned.1.call-update) | async-done | bytes 65552 | tf_op jit(solution)/shard_map/reduce_scatter | solution.py:209
  435.7 1.7 copy.188
  437.4 3.8 fusion.58
  443.3 4.9 all-to-all-start.13
  448.2 126.4 %reduce-scatter.15.cloned.1.call-done = bf16[32,3072]{1,0:T(8,128)(2,1)} async-done(((bf16[1024,3072]{1,0:T(8,128)(2,1)}), bf16[32,3072]{1,0:T(8,128)(2,1)}) %reduce-scatter.15.cloned.1.call-update) | async-done | bytes 196624 | tf_op jit(solution)/shard_map/reduce_scatter | solution.py:206
  574.6 2.2 copy.186
  576.8 10.1 %fusion.64 = bf16[2,880,1,64]{1,3,0,2:T(8,128)(2,1)S(1)} fusion(bf16[2,880,64]{1,2,0:T(8,128)(2,1)S(1)} %reshape_transpose.13, f32[2,880,880]{1,2,0:T(8,128)} %fusion.108, f32[2,880,880]{1,2,0:T(8,128)} %get-tuple-element.40, f32[2,880]{1,0:T(2,128)S(1)} %get-tuple-element.39), kind=kOutput, calls=%fused_computation.51 | convolution fusion | flops 209203280 | bytes 12848000 | tf_op jit(solution)/shard_map/rtl,rlp->rtp/dot_general | solution.py:50
  588.6 4.9 all-to-all-start.11
  596.2 4.8 all-to-all-done.11
  604.7 1.8 copy.173
  606.5 9.9 %reduce-scatter.13.cloned.1.call-done = bf16[16,128]{0,1:T(8,128)(2,1)} async-done(((bf16[16,1024]{0,1:T(8,128)(2,1)}), bf16[16,128]{0,1:T(8,128)(2,1)}) %reduce-scatter.13.cloned.1.call-update) | async-done | bytes 4112 | tf_op jit(solution)/shard_map/reduce_scatter | solution.py:214
  617.8 39.3 %reduce-scatter.23.cloned.1.call-done = bf16[128,32]{1,0:T(8,128)(2,1)} async-done(((bf16[1024,32]{1,0:T(8,128)(2,1)}), bf16[128,32]{1,0:T(8,128)(2,1)}) %reduce-scatter.23.cloned.1.call-update) | async-done | bytes 8208
  658.5 40.5 %reduce-scatter.21.cloned.1.call-done = bf16[384,32]{1,0:T(8,128)(2,1)} async-done(((bf16[3072,32]{1,0:T(8,128)(2,1)}), bf16[384,32]{1,0:T(8,128)(2,1)}) %reduce-scatter.21.cloned.1.call-update) | async-done | bytes 24592
  (152 shorter events, 66.4 us)
Async XLA Ops:
  7.2 1.7 copy-start
  8.9 1.7 copy-start.9
  10.6 14.0 %copy-start.22 = (s32[2]{0:T(128)S(1)}, s32[2]{0:T(128)}, u32[]{:S(2)}) copy-start(s32[2]{0:T(128)} %param.19) | copy-start | bytes 28
  10.6 14.0 %copy-start.2 = (bf16[2,110,1024]{2,0,1:T(2,128)(2,1)S(1)}, bf16[2,110,1024]{2,0,1:T(2,128)(2,1)}, u32[]{:S(2)}) copy-start(bf16[2,110,1024]{2,0,1:T(2,128)(2,1)} %param.11) | copy-start | bytes 1351684
  10.6 14.3 %copy-start.16 = (bf16[256,1024]{1,0:T(8,128)(2,1)S(1)}, bf16[256,1024]{1,0:T(8,128)(2,1)}, u32[]{:S(2)}) copy-start(bf16[256,1024]{1,0:T(8,128)(2,1)} %param.18) | copy-start | bytes 1572868
  12.9 28.0 %all-to-all-start.2 = ((bf16[32,2,3520]{2,1,0:T(2,128)(2,1)}), bf16[32,2,3520]{2,1,0:T(2,128)(2,1)}, u32[]{:S(2)}, u32[]{:S(2)}) async-start(bf16[32,2,3520]{2,1,0:T(2,128)(2,1)} %reshape.141), calls=%async_computation.2 | async-start | bytes 917504 | tf_op jit(solution)/shard_map/all_to_all | solution.py:113
  25.4 5.7 copy-start.7
  40.9 23.3 %all-to-all-start = ((bf16[32,2,3520]{2,1,0:T(2,128)(2,1)}), bf16[32,2,3520]{2,1,0:T(2,128)(2,1)S(1)}, u32[]{:S(2)}, u32[]{:S(2)}) async-start(bf16[32,2,3520]{2,1,0:T(2,128)(2,1)} %reshape.145), calls=%async_computation | async-start | bytes 917504 | tf_op jit(solution)/shard_map/all_to_all | solution.py:104
  50.2 21.3 %copy-start.20 = (s32[64,4]{0,1:T(4,128)S(1)}, s32[64,4]{0,1:T(4,128)}, u32[]{:S(2)}) copy-start(s32[64,4]{0,1:T(4,128)} %param.21) | copy-start | bytes 3076
  50.2 40.6 %copy-start.21 = (s32[64]{0:T(128)S(1)}, s32[64]{0:T(128)}, u32[]{:S(2)}) copy-start(s32[64]{0:T(128)} %param.20) | copy-start | bytes 772
  64.2 21.3 %all-to-all-start.3 = ((bf16[32,2,3520]{2,1,0:T(2,128)(2,1)}), bf16[32,2,3520]{2,1,0:T(2,128)(2,1)S(1)}, u32[]{:S(2)}, u32[]{:S(2)}) async-start(bf16[32,2,3520]{2,1,0:T(2,128)(2,1)} %reshape.143), calls=%async_computation.3 | async-start | bytes 917504 | tf_op jit(solution)/shard_map/all_to_all | solution.py:110
  85.5 21.5 %all-to-all-start.1 = ((bf16[32,2,3520]{2,1,0:T(2,128)(2,1)}), bf16[32,2,3520]{2,1,0:T(2,128)(2,1)S(1)}, u32[]{:S(2)}, u32[]{:S(2)}) async-start(bf16[32,2,3520]{2,1,0:T(2,128)(2,1)} %reshape.139), calls=%async_computation.1 | async-start | bytes 917504 | tf_op jit(solution)/shard_map/all_to_all | solution.py:107
  101.2 8.2 %copy-start.5 = (bf16[32,2,1,55,64]{4,1,0,3,2:T(2,128)(2,1)}, bf16[32,2,1,55,64]{4,1,0,3,2:T(2,128)(2,1)S(1)}, u32[]{:S(2)}) copy-start(bf16[32,2,1,55,64]{4,1,0,3,2:T(2,128)(2,1)S(1)} %copy.139) | copy-start | bytes 1351684
  109.4 5.1 copy-start.12
  111.2 3.2 copy-start.14
  120.2 21.7 %all-to-all-start.5 = ((bf16[32,2,3520]{2,1,0:T(2,128)(2,1)}), bf16[32,2,3520]{2,1,0:T(2,128)(2,1)S(1)}, u32[]{:S(2)}, u32[]{:S(2)}) async-start(bf16[32,2,3520]{2,1,0:T(2,128)(2,1)} %reshape.149), calls=%async_computation.5 | async-start | bytes 917504 | tf_op jit(solution)/shard_map/all_to_all | solution.py:134
  127.6 19.3 %copy-start.13 = (bf16[32,2,1,55,64]{4,1,0,3,2:T(2,128)(2,1)S(1)}, bf16[32,2,1,55,64]{4,1,0,3,2:T(2,128)(2,1)}, u32[]{:S(2)}) copy-start(bf16[32,2,1,55,64]{4,1,0,3,2:T(2,128)(2,1)} %copy-done.12) | copy-start | bytes 1351684
  141.9 21.3 %all-to-all-start.6 = ((bf16[32,2,3520]{2,1,0:T(2,128)(2,1)}), bf16[32,2,3520]{2,1,0:T(2,128)(2,1)S(1)}, u32[]{:S(2)}, u32[]{:S(2)}) async-start(bf16[32,2,3520]{2,1,0:T(2,128)(2,1)} %reshape.151), calls=%async_computation.6 | async-start | bytes 917504 | tf_op jit(solution)/shard_map/all_to_all | solution.py:135
  163.2 21.3 %all-to-all-start.4 = ((bf16[32,2,3520]{2,1,0:T(2,128)(2,1)}), bf16[32,2,3520]{2,1,0:T(2,128)(2,1)S(1)}, u32[]{:S(2)}, u32[]{:S(2)}) async-start(bf16[32,2,3520]{2,1,0:T(2,128)(2,1)} %reshape.147), calls=%async_computation.4 | async-start | bytes 917504 | tf_op jit(solution)/shard_map/all_to_all | solution.py:133
  168.2 145.5 %reduce-scatter.19.cloned.1.call-start = ((), (), s32[]{:S(2)}) async-start(), calls=%async_computation.24 | async-start | bytes 1081344
  186.6 2.8 copy-start.6
  189.7 3.4 copy-start.3
  193.1 5.4 copy-start.4
  193.1 5.4 copy-start.10
  198.4 0.9 copy-start.17
  203.2 232.6 %reduce-scatter.17.cloned.1.call-start = ((), (), s32[]{:S(2)}) async-start(), calls=%async_computation.23 | async-start | bytes 2162688 | tf_op jit(solution)/shard_map/reduce_scatter | solution.py:209
  242.2 332.4 %reduce-scatter.15.cloned.1.call-start = ((), (), s32[]{:S(2)}) async-start(), calls=%async_computation.22 | async-start | bytes 6488064 | tf_op jit(solution)/shard_map/reduce_scatter | solution.py:206
  246.1 2.7 copy-start.8
  253.4 1.1 copy-start.15
  256.1 11.9 %all-to-all-start.8 = ((bf16[2,110,8,64]{1,3,0,2:T(8,128)(2,1)}), bf16[2,110,8,64]{1,3,0,2:T(8,128)(2,1)S(1)}, u32[]{:S(2)}, u32[]{:S(2)}) async-start(bf16[2,110,8,64]{1,3,0,2:T(8,128)(2,1)} %copy.152), calls=%async_computation.8 | async-start | bytes 524288 | tf_op jit(solution)/shard_map/all_to_all | solution.py:171
  268.1 10.3 %all-to-all-start.7 = ((bf16[2,110,8,64]{1,3,0,2:T(8,128)(2,1)}), bf16[2,110,8,64]{1,3,0,2:T(8,128)(2,1)S(1)}, u32[]{:S(2)}, u32[]{:S(2)}) async-start(bf16[2,110,8,64]{1,3,0,2:T(8,128)(2,1)} %copy.150), calls=%async_computation.7 | async-start | bytes 524288 | tf_op jit(solution)/shard_map/all_to_all | solution.py:170
  271.5 10.8 %copy-start.11 = (bf16[512,1024]{1,0:T(8,128)(2,1)S(1)}, bf16[512,1024]{1,0:T(8,128)(2,1)}, u32[]{:S(2)}) copy-start(bf16[512,1024]{1,0:T(8,128)(2,1)} %param.15) | copy-start | bytes 3145732
  278.3 10.3 %all-to-all-start.10 = ((bf16[2,110,8,64]{1,3,0,2:T(8,128)(2,1)}), bf16[2,110,8,64]{1,3,0,2:T(8,128)(2,1)S(1)}, u32[]{:S(2)}, u32[]{:S(2)}) async-start(bf16[2,110,8,64]{1,3,0,2:T(8,128)(2,1)} %copy.156), calls=%async_computation.10 | async-start | bytes 524288 | tf_op jit(solution)/shard_map/all_to_all | solution.py:172
  282.2 14.6 %copy-start.18 = (bf16[2,880,64]{1,2,0:T(8,128)(2,1)}, bf16[2,880,64]{1,2,0:T(8,128)(2,1)S(1)}, u32[]{:S(2)}) copy-start(bf16[2,880,64]{1,2,0:T(8,128)(2,1)S(1)} %reshape_transpose.12) | copy-start | bytes 675844
  288.6 10.3 %all-to-all-start.9 = ((bf16[2,110,8,64]{1,0,3,2:T(2,128)(2,1)}), bf16[2,110,8,64]{1,0,3,2:T(2,128)(2,1)S(1)}, u32[]{:S(2)}, u32[]{:S(2)}) async-start(bf16[2,110,8,64]{1,0,3,2:T(2,128)(2,1)} %reshape.126), calls=%async_computation.9 | async-start | bytes 524288 | tf_op jit(solution)/shard_map/all_to_all | solution.py:173
  292.1 324.3 %reduce-scatter.13.cloned.1.call-start = ((), (), s32[]{:S(2)}) async-start(), calls=%async_computation.21 | async-start | bytes 294912 | tf_op jit(solution)/shard_map/reduce_scatter | solution.py:214
  299.3 15.9 %copy-start.19 = (bf16[2,880,64]{1,2,0:T(8,128)(2,1)S(1)}, bf16[2,880,64]{1,2,0:T(8,128)(2,1)}, u32[]{:S(2)}) copy-start(bf16[2,880,64]{1,2,0:T(8,128)(2,1)} %copy-done.18) | copy-start | bytes 675844
  327.1 116.1 %all-to-all-start.12 = ((bf16[8,2,7040]{2,1,0:T(2,128)(2,1)}), bf16[8,2,7040]{2,1,0:T(2,128)(2,1)S(1)}, u32[]{:S(2)}, u32[]{:S(2)}) async-start(bf16[8,2,7040]{2,1,0:T(2,128)(2,1)} %reshape.155), calls=%async_computation.12 | async-start | bytes 450560 | tf_op jit(solution)/shard_map/all_to_all | solution.py:196
  332.0 325.0 %reduce-scatter.23.cloned.1.call-start = ((), (), s32[]{:S(2)}) async-start(), calls=%async_computation.26 | async-start | bytes 294912
  443.3 145.4 %all-to-all-start.13 = ((bf16[8,2,7040]{2,1,0:T(2,128)(2,1)}), bf16[8,2,7040]{2,1,0:T(2,128)(2,1)S(1)}, u32[]{:S(2)}, u32[]{:S(2)}) async-start(bf16[8,2,7040]{2,1,0:T(2,128)(2,1)} %reshape.153), calls=%async_computation.13 | async-start | bytes 450560 | tf_op jit(solution)/shard_map/all_to_all | solution.py:197
  448.2 250.8 %reduce-scatter.21.cloned.1.call-start = ((), (), s32[]{:S(2)}) async-start(), calls=%async_computation.25 | async-start | bytes 884736
  588.6 12.4 %all-to-all-start.11 = ((bf16[8,2,7040]{2,1,0:T(2,128)(2,1)}), bf16[8,2,7040]{2,1,0:T(2,128)(2,1)}, u32[]{:S(2)}, u32[]{:S(2)}) async-start(bf16[8,2,7040]{2,1,0:T(2,128)(2,1)} %reshape.157), calls=%async_computation.11 | async-start | bytes 450560 | tf_op jit(solution)/shard_map/all_to_all | solution.py:195
  601.0 99.5 %copy-start.1 = (bf16[1024,1024]{1,0:T(8,128)(2,1)S(1)}, bf16[1024,1024]{1,0:T(8,128)(2,1)}, u32[]{:S(2)}) copy-start(bf16[1024,1024]{1,0:T(8,128)(2,1)} %param.17) | copy-start | bytes 6291460
Sparse Core Ops, SparseCore 0:
  203.3 110.3 reduce-scatter.18
  318.3 117.3 reduce-scatter.16
  440.0 134.5 reduce-scatter.14
  577.0 39.3 reduce-scatter.12
  618.8 38.1 reduce-scatter.22
  659.4 39.4 reduce-scatter.20
where the time goes:
time: 718 us; the launch traced here: 708 us
  waiting for transfers between devices  423 us (59%)
  local copies, waits for them, and re-layouts  98.4 us (14%)
  starting transfers between devices  74.6 us (10%)
  matrix products  71.7 us (10%)
  blocking collectives  21.4 us (3%)
  between operations  15.4 us (2%)
    reduce_scatter x1, waiting for transfers between devices, shards(): lax.psum_scatter(term_qkv_temporal.astype(jnp.bfloat16), 'frame', scatter...  126 us
    reduce_scatter x1, waiting for transfers between devices, shards(): lax.psum_scatter(term_proj_temporal.astype(jnp.bfloat16), 'frame', scatte...  104 us
    unnamed x9, waiting for transfers between devices  90.5 us
    unnamed x81, local copies, waits for them, and re-layouts  48.6 us
    all_to_all x1, blocking collectives, shards(): lax.all_to_all(frame_major(outcome[0]), 'frame', split_axis=0, concat_axi...  21.4 us
    dot_general x2, matrix products, attend_grad(): jnp.einsum('rtl,rlp->rtp', score_gradient, key_matrix_rows, preferred_ele...  14.9 us
  transfers between devices with their start and end apart: 20, of which 18 were waited for; matrix products, arithmetic and copies ran while one was open for 19% of the time, Pallas kernels for 0%

commit v1 on v0

v1 whole, which is shorter than its diff:
```python
import functools

import jax
import jax.numpy as jnp
from jax import lax
from jax.experimental import pallas as pl
from jax.experimental.pallas import tpu as pltpu
from jax.sharding import PartitionSpec as P

MESH = pl.DeviceIdType.MESH
F32 = jnp.float32
BF16 = jnp.bfloat16
D = 1024
E = 64
F = 64
NF = 32
NP = 8
TOK = 110
PAD = 112
SLOT = 4
BUSY = 28
ROWS = F * SLOT
SP = NP * PAD
SCALE = E ** (-0.5)
NEG = -1e30
VLIMIT = 56 * 1024 * 1024


def frame_embedding(noise_steps, embed_width):
    half_width = embed_width // 2
    counter = jnp.arange(half_width, dtype=jnp.float32)
    frequency = jnp.exp(-jnp.log(10000.0) * counter / half_width)
    angles = noise_steps.astype(jnp.float32)[:, None] * frequency[None, :]
    return jnp.concatenate([jnp.cos(angles), jnp.sin(angles)], axis=1)


def visible_frames(positions, memory):
    frame_total = positions.shape[0]
    earlier = positions[None, :] <= positions[:, None]
    frame_ids = jnp.arange(frame_total, dtype=jnp.int32)
    recalled = jnp.any(memory[:, :, None] == frame_ids[None, None, :], axis=1)
    return jnp.logical_or(earlier, recalled)


def rcopy(src, dst, ssem, rsem, f, p):
    return pltpu.make_async_remote_copy(
        src_ref=src, dst_ref=dst, send_sem=ssem, recv_sem=rsem, device_id=(f, p), device_id_type=MESH
    )


def barrier(me_f, me_p, frame, patch):
    sem = pltpu.get_barrier_semaphore()
    count = 0
    if frame:

        def greet(k, _):
            pl.semaphore_signal(sem, inc=1, device_id=(lax.rem(me_f + k, NF), me_p), device_id_type=MESH)
            return 0

        lax.fori_loop(1, NF, greet, 0)
        count += NF - 1
    if patch:

        def greet_p(k, _):
            pl.semaphore_signal(sem, inc=1, device_id=(me_f, lax.rem(me_p + k, NP)), device_id_type=MESH)
            return 0

        lax.fori_loop(1, NP, greet_p, 0)
        count += NP - 1
    pl.semaphore_wait(sem, count)


def low_rows():
    return lax.broadcasted_iota(jnp.int32, (8, D), 0) < 4


def swap_halves(a, b, low):
    return jnp.where(low, a, pltpu.roll(b, 4, 0)), jnp.where(low, pltpu.roll(a, 4, 0), b)


def swap_lanes(a, b):
    low = lax.broadcasted_iota(jnp.int32, a.shape, 1) < E
    return jnp.where(low, a, pltpu.roll(b, E, 1)), jnp.where(low, pltpu.roll(a, E, 1), b)


def forward_kernel(
    stream, upstream, gain, sqkv, recv, recv_s, nbuf, ubuf, send, send_s, ssem, rsem, ssem_s, rsem_s, lsem
):
    me_f, me_p = lax.axis_index("frame"), lax.axis_index("patch")
    for f in range(2):
        x = stream[f].astype(F32)
        inverse = lax.rsqrt(jnp.mean(x * x, axis=-1, keepdims=True) + 1e-06)
        nbuf[f, 104:128] = jnp.zeros((24, D), F32)
        ubuf[f, 104:128] = jnp.zeros((24, D), F32)
        nbuf[f, 0:TOK] = x * inverse * gain[f : f + 1]
        ubuf[f, 0:TOK] = upstream[f].astype(F32)

    low = low_rows()

    def pack(i, _):
        rows = pl.ds(pl.multiple_of(i * 8, 8), 8)
        n0, n1 = swap_halves(nbuf[0, rows], nbuf[1, rows], low)
        u0, u1 = swap_halves(ubuf[0, rows], ubuf[1, rows], low)
        send[2 * i] = jnp.concatenate([n0, u0], axis=0).astype(BF16)
        send[2 * i + 1] = jnp.concatenate([n1, u1], axis=0).astype(BF16)
        return 0

    lax.fori_loop(0, BUSY // 2, pack, 0)

    @pl.when(me_f >= BUSY)
    def _():
        recv[...] = jnp.zeros(recv.shape, BF16)

    barrier(me_f, me_p, True, True)

    def copy_to(k):
        d = lax.rem(me_f + k, NF)
        return d, rcopy(send.at[d], recv.at[me_f], ssem.at[k], rsem.at[k], d, me_p)

    def start(k, _):
        d, copy = copy_to(k)

        @pl.when(d < BUSY)
        def _():
            copy.start()

        return 0

    lax.fori_loop(1, NF, start, 0)
    local = pltpu.make_async_copy(send.at[me_f], recv.at[me_f], lsem.at[0])

    @pl.when(me_f < BUSY)
    def _():
        local.start()

    send_s[:, :, 96:PAD] = jnp.zeros((NP, 3, 16, 128), BF16)
    for j in range(4):
        v = []
        for f in range(2):
            a = sqkv[f, :, 128 * j : 128 * j + 128].astype(F32)
            b = sqkv[f, :, 512 + 128 * j : 640 + 128 * j].astype(F32)
            m0, m1 = swap_lanes(a, b)
            send_s[2 * j, f, 0:TOK] = m0.astype(BF16)
            send_s[2 * j + 1, f, 0:TOK] = m1.astype(BF16)
            v.append(sqkv[f, :, 1024 + 128 * j : 1152 + 128 * j].astype(F32))
        m0, m1 = swap_lanes(v[0], v[1])
        send_s[2 * j, 2, 0:TOK] = m0.astype(BF16)
        send_s[2 * j + 1, 2, 0:TOK] = m1.astype(BF16)

    def copy_s(k):
        d = lax.rem(me_p + k, NP)
        return rcopy(send_s.at[d], recv_s.at[me_p], ssem_s.at[k], rsem_s.at[k], me_f, d)

    def start_s(k, _):
        copy_s(k).start()
        return 0

    lax.fori_loop(1, NP, start_s, 0)
    recv_s[me_p] = send_s[me_p]

    @pl.when(me_f < BUSY)
    def _():
        local.wait()

    def finish(k, _):
        d, copy = copy_to(k)

        @pl.when(d < BUSY)
        def _():
            copy.wait_send()

        @pl.when(me_f < BUSY)
        def _():
            copy.wait_recv()

        return 0

    lax.fori_loop(1, NF, finish, 0)

    def finish_s(k, _):
        copy_s(k).wait()
        return 0

    lax.fori_loop(1, NP, finish_s, 0)


def dot(a, b, da, db):
    return lax.dot_general(a, b, (((da,), (db,)), ((), ())), preferred_element_type=F32)


def temporal_kernel(recv, wqkv, wp, bias, term_a, term_b, gn, nv, uv, nt, proj, g, o, dqkv, ot):
    x = recv[...].astype(F32)
    nv[...] = x[:, 0:8].reshape(ROWS, D).astype(BF16)
    uv[...] = x[:, 8:16].reshape(ROWS, D).astype(BF16)
    nt[...] = nv[...].T

    def project(c, _):
        cols = pl.ds(pl.multiple_of(c * 512, 512), 512)
        proj[:, cols] = dot(nv[...], wqkv[:, cols], 1, 0).astype(BF16)
        return 0

    lax.fori_loop(0, 6, project, 0)

    def project_g(c, _):
        cols = pl.ds(pl.multiple_of(c * 512, 512), 512)
        g[:, cols] = dot(uv[...], wp[cols, :], 1, 1).astype(BF16)
        return 0

    lax.fori_loop(0, 2, project_g, 0)
    low = lax.broadcasted_iota(jnp.int32, (ROWS, 128), 1) < E

    def pair(j, _):
        def cols(base):
            return pl.ds(pl.multiple_of(base + j * 128, 128), 128)

        qp, kp, vp, gp = proj[:, cols(0)], proj[:, cols(D)], proj[:, cols(2 * D)], g[:, cols(0)]
        parts = []
        for half in range(2):
            mine = low if half == 0 else jnp.logical_not(low)
            zero = jnp.zeros_like(qp)
            kh = jnp.where(mine, kp, zero)
            vh = jnp.where(mine, vp, zero)
            st = dot(kh, qp, 1, 1) * SCALE + bias[...]
            e = jnp.exp(st - jnp.max(st, axis=0, keepdims=True))
            p = e / jnp.sum(e, axis=0, keepdims=True)
            pb = p.astype(BF16)
            dp = dot(vh, gp, 1, 1)
            ds = (p * (dp - jnp.sum(p * dp, axis=0, keepdims=True)) * SCALE).astype(BF16)
            parts.append(
                (dot(pb, vp, 0, 0), dot(ds, kp, 0, 0), dot(ds, qp, 1, 0), dot(pb, gp, 1, 0))
            )
        out = [jnp.where(low, a, b).astype(BF16) for a, b in zip(*parts)]
        o[:, cols(0)] = out[0]
        dqkv[:, cols(0)] = out[1]
        dqkv[:, cols(D)] = out[2]
        dqkv[:, cols(2 * D)] = out[3]
        return 0

    lax.fori_loop(0, 8, pair, 0)
    back = dot(dqkv[...], wqkv[...], 1, 1).reshape(NF, 8, D)
    gn[...] = jnp.concatenate([back[:, :, 0:512], back[:, :, 512:1024]], axis=1).astype(BF16)
    ot[...] = o[...].T

    def weights(p, _):
        r = dot(nt[...], dqkv[:, pl.ds(pl.multiple_of(p * 384, 128), 384)], 1, 0)
        r = r.reshape(16, 2, 32, 384)
        term_a[:, :, p, :, 0:384] = r[:, :, 0:16].astype(BF16)
        term_b[:, :, p, :, 0:384] = r[:, :, 16:32].astype(BF16)
        s = dot(ot[...], uv[:, pl.ds(pl.multiple_of(p * 128, 128), 128)], 1, 0)
        s = s.reshape(16, 2, 32, 128)
        term_a[:, :, p, :, 384:512] = s[:, :, 0:16].astype(BF16)
        term_b[:, :, p, :, 384:512] = s[:, :, 16:32].astype(BF16)
        return 0

    lax.fori_loop(0, NP, weights, 0)


def back_kernel(
    gn, stream, upstream, gain, wps, so, gs_out, recv_g, term_p,
    recv, sbuf, sopad, send_g, ssem, rsem, ssem_g, rsem_g, lsem,
):
    me_f, me_p = lax.axis_index("frame"), lax.axis_index("patch")
    barrier(me_f, me_p, True, True)

    def copy_to(k):
        d = lax.rem(me_f + k, NF)
        return rcopy(gn.at[d], recv.at[me_f], ssem.at[k], rsem.at[k], d, me_p)

    def start(k, _):
        copy_to(k).start()
        return 0

    local = pltpu.make_async_copy(gn.at[me_f], recv.at[me_f], lsem.at[0])

    @pl.when(me_f < BUSY)
    def _():
        lax.fori_loop(1, NF, start, 0)
        local.start()

    for f in range(2):
        sopad[f, 96:PAD] = jnp.zeros((16, 512), BF16)
        sopad[f, 0:TOK] = so[f]

    def land(k, _):
        @pl.when(lax.rem(me_f + NF - k, NF) < BUSY)
        def _():
            copy_to(k).wait_recv()

        return 0

    lax.fori_loop(1, NF, land, 0)

    @pl.when(me_f < BUSY)
    def _():
        local.wait()

    low = low_rows()

    def unpack(i, _):
        rows = pl.ds(pl.multiple_of(i * 8, 8), 8)
        x = recv[2 * i].astype(F32)
        y = recv[2 * i + 1].astype(F32)
        x = jnp.concatenate([x[0:8], x[8:16]], axis=1)
        y = jnp.concatenate([y[0:8], y[8:16]], axis=1)
        sbuf[0, rows], sbuf[1, rows] = swap_halves(x, y, low)
        return 0

    lax.fori_loop(0, BUSY // 2, unpack, 0)
    for f in range(2):
        x = stream[f].astype(F32)
        inverse = lax.rsqrt(jnp.mean(x * x, axis=-1, keepdims=True) + 1e-06)
        scaled = sbuf[f, 0:TOK] * gain[f : f + 1]
        inner = jnp.mean(x * scaled, axis=-1, keepdims=True)
        out = upstream[f].astype(F32) + inverse * scaled - x * (inverse * inverse * inverse) * inner
        gs_out[f] = out.astype(BF16)
        sbuf[f, 104:PAD] = jnp.zeros((8, D), F32)
        sbuf[f, 0:TOK] = out
    gs = sbuf[...].reshape(2 * PAD, D).astype(BF16)
    gos = dot(gs, wps[...], 1, 1)
    for j in range(4):
        cols = slice(128 * j, 128 * j + 128)
        m0, m1 = swap_lanes(gos[0:PAD, cols], gos[PAD : 2 * PAD, cols])
        send_g[2 * j] = m0.astype(BF16)
        send_g[2 * j + 1] = m1.astype(BF16)

    def copy_g(k):
        d = lax.rem(me_p + k, NP)
        return rcopy(send_g.at[d], recv_g.at[me_p], ssem_g.at[k], rsem_g.at[k], me_f, d)

    def start_g(k, _):
        copy_g(k).start()
        return 0

    lax.fori_loop(1, NP, start_g, 0)
    recv_g[me_p] = send_g[me_p]
    tp = dot(sopad[...].reshape(2 * PAD, 512), gs, 0, 0)
    for p in range(NP):
        term_p[:, :, p] = tp[:, 128 * p : 128 * p + 128].reshape(16, 2, 16, 128).astype(BF16)

    def gone(k, _):
        copy_to(k).wait_send()
        return 0

    @pl.when(me_f < BUSY)
    def _():
        lax.fori_loop(1, NF, gone, 0)

    def finish_g(k, _):
        copy_g(k).wait()
        return 0

    lax.fori_loop(1, NP, finish_g, 0)


def spatial_kernel(qkv, gg, out, kq, vz, acc_k, acc_q, acc_v, send, recv, ssem, rsem):
    me_f, me_p = lax.axis_index("frame"), lax.axis_index("patch")
    barrier(me_f, me_p, False, True)
    low = lax.broadcasted_iota(jnp.int32, (SP, 128), 1) < E
    dead = lax.rem(lax.broadcasted_iota(jnp.int32, (SP, 128), 0), PAD) >= TOK
    bias = jnp.where(dead, NEG, 0.0).astype(F32)
    vv = qkv[:, 2].reshape(SP, 128).astype(F32)
    for f in range(2):
        x = qkv[:, f].reshape(SP, 128).astype(F32)
        kq[...] = jnp.where(low, pltpu.roll(x, E, 1), 0.0).astype(BF16)
        vz[...] = jnp.where(low if f == 0 else jnp.logical_not(low), vv, 0.0).astype(BF16)
        acc_k[...] = jnp.zeros((SP, 128), F32)
        acc_v[f] = jnp.zeros((SP, 128), F32)
        qk = x.astype(BF16)
        g_all = gg[...].reshape(SP, 128)
        for b in range(SP // 128):
            rows = slice(b * 128, b * 128 + 128)
            q_rows, g_rows = qk[rows], g_all[rows]
            st = dot(kq[...], q_rows, 1, 1) * SCALE + bias
            e = jnp.exp(st - jnp.max(st, axis=0, keepdims=True))
            p = e / jnp.sum(e, axis=0, keepdims=True)
            dp = dot(vz[...], g_rows, 1, 1)
            ds = (p * (dp - jnp.sum(p * dp, axis=0, keepdims=True)) * SCALE).astype(BF16)
            acc_v[f] += dot(p.astype(BF16), g_rows, 1, 0)
            acc_k[...] += dot(ds, q_rows, 1, 0)
            acc_q[rows] = dot(ds, qk, 0, 0)
        send[:, f] = jnp.where(low, acc_k[...], acc_q[...]).astype(BF16).reshape(NP, PAD, 128)
    send[:, 2] = jnp.where(low, acc_v[0], acc_v[1]).astype(BF16).reshape(NP, PAD, 128)

    def copy_to(k):
        d = lax.rem(me_p + k, NP)
        return rcopy(send.at[d], recv.at[me_p], ssem.at[k], rsem.at[k], me_f, d)

    def start(k, _):
        copy_to(k).start()
        return 0

    lax.fori_loop(1, NP, start, 0)
    recv[me_p] = send[me_p]

    def finish(k, _):
        copy_to(k).wait()
        return 0

    lax.fori_loop(1, NP, finish, 0)
    for j in range(4):
        c = 128 * j
        for f in range(2):
            k, q = swap_lanes(recv[2 * j, f].astype(F32), recv[2 * j + 1, f].astype(F32))
            out[f, :, c : c + 128] = q[0:TOK].astype(BF16)
            out[f, :, 512 + c : 640 + c] = k[0:TOK].astype(BF16)
        v0, v1 = swap_lanes(recv[2 * j, 2].astype(F32), recv[2 * j + 1, 2].astype(F32))
        out[0, :, 1024 + c : 1152 + c] = v0[0:TOK].astype(BF16)
        out[1, :, 1024 + c : 1152 + c] = v1[0:TOK].astype(BF16)


def place():
    me_f, me_p = lax.axis_index("frame"), lax.axis_index("patch")
    z, y_hi, core = me_f // 4, lax.rem(me_f // 2, 2), lax.rem(me_f, 2)
    x, y_lo = me_p // 2, lax.rem(me_p, 2)
    return z, y_hi, core, x, y_lo


def device(z, y, core, x):
    return z * 4 + (y // 2) * 2 + core, x * 2 + lax.rem(y, 2)


def sum_barrier():
    z, y_hi, core, x, y_lo = place()
    y = y_hi * 2 + y_lo
    sem = pltpu.get_barrier_semaphore()

    def greet(f, p):
        pl.semaphore_signal(sem, inc=1, device_id=(f, p), device_id_type=MESH)

    greet(*device(z, y, 1 - core, x))
    for k in range(1, 4):
        greet(*device(z, y, core, lax.rem(x + k, 4)))
        greet(*device(z, lax.rem(y + k, 4), core, x))
    for k in range(1, 8):
        greet(*device(lax.rem(z + k, 8), y, core, x))
    pl.semaphore_wait(sem, 14)


class Sum:
    def __init__(self, term, bufs, sems, x_first):
        self.term, self.x_first = term, x_first
        self.r0, self.t1, self.r1, self.t2, self.r2, self.t3, self.r3 = bufs
        self.ssem, self.rsem = sems
        self.z, self.y_hi, self.core, self.x, self.y_lo = place()
        self.y = self.y_hi * 2 + self.y_lo
        self.cols = term.shape[-1]

    def copies(self, stage):
        out = []
        if stage == 0:
            dst = device(self.z, self.y, 1 - self.core, self.x)
            return [rcopy(self.term.at[:, 1 - self.core], self.r0, self.ssem.at[0], self.rsem.at[0], *dst)]
        n = 8 if stage == 3 else 4
        first = {1: 1, 2: 4, 3: 7}[stage]
        for k in range(1, n):
            along_x = (stage == 1) == self.x_first
            if stage == 3:
                to = lax.rem(self.z + k, 8)
                src, dst, where = self.t3.at[to], self.r3.at[k - 1], device(to, self.y, self.core, self.x)
            elif along_x:
                to = lax.rem(self.x + k, 4)
                where = device(self.z, self.y, self.core, to)
                if stage == 1:
                    src, dst = self.t1.at[:, :, to], self.r1.at[k - 1]
                else:
                    src, dst = self.t2.at[:, to], self.r2.at[k - 1]
            else:
                to = lax.rem(self.y + k, 4)
                where = device(self.z, to, self.core, self.x)
                if stage == 1:
                    src, dst = self.t1.at[:, to // 2, :, lax.rem(to, 2)], self.r1.at[k - 1]
                else:
                    src, dst = self.t2.at[:, to // 2, lax.rem(to, 2)], self.r2.at[k - 1]
            s = first + k - 1
            out.append(rcopy(src, dst, self.ssem.at[s], self.rsem.at[s], *where))
        return out

    def start(self, stage):
        for c in self.copies(stage):
            c.start()

    def land(self, stage):
        for c in self.copies(stage):
            c.wait_recv()

    def gone(self):
        for stage in range(4):
            for c in self.copies(stage):
                c.wait_send()

    def add0(self):
        shape = (4, 2, 16, self.cols)

        def body(i, _):
            total = self.term[i, self.core].astype(F32) + self.r0[i].astype(F32)
            self.t1[i // 2, lax.rem(i, 2)] = total.astype(BF16).reshape(shape)
            return 0

        lax.fori_loop(0, 16, body, 0)

    def add1(self):
        def body(i, _):
            if self.x_first:
                total = self.t1[i, :, self.x].astype(F32)
            else:
                total = self.t1[i, self.y_hi, :, self.y_lo].astype(F32)
            for k in range(3):
                total = total + self.r1[k, i].astype(F32)
            self.t2[i] = total.astype(BF16)
            return 0

        lax.fori_loop(0, 8, body, 0)

    def add2(self):
        def body(i, _):
            if self.x_first:
                total = self.t2[i, self.y_hi, self.y_lo].astype(F32)
            else:
                total = self.t2[i, self.x].astype(F32)
            for k in range(3):
                total = total + self.r2[k, i].astype(F32)
            self.t3[i] = total.astype(BF16)
            return 0

        lax.fori_loop(0, 8, body, 0)

    def add3(self):
        total = self.t3[self.z].astype(F32)
        for k in range(7):
            total = total + self.r3[k].astype(F32)
        return total


def sum_scratch(cols, x_first):
    mid = (2, 2) if x_first else (4,)
    return [
        pltpu.VMEM((16, NP, 16, cols), BF16),
        pltpu.VMEM((8, 2, 4, 2, 16, cols), BF16),
        pltpu.VMEM((3, 8) + mid + (16, cols), BF16),
        pltpu.VMEM((8,) + mid + (16, cols), BF16),
        pltpu.VMEM((3, 8, 16, cols), BF16),
        pltpu.VMEM((8, 16, cols), BF16),
        pltpu.VMEM((7, 16, cols), BF16),
        pltpu.SemaphoreType.DMA((14,)),
        pltpu.SemaphoreType.DMA((14,)),
    ]


def sum_kernel(term_a, term_b, term_p, out_q, out_t, out_s, *scratch):
    sums = [
        Sum(term, scratch[9 * i : 9 * i + 7], scratch[9 * i + 7 : 9 * i + 9], x_first)
        for i, (term, x_first) in enumerate(((term_a, True), (term_b, False), (term_p, True)))
    ]
    sum_barrier()
    for s in sums:
        s.start(0)
    for s in sums:
        s.land(0)
        s.add0()
        s.start(1)
    for s in sums:
        s.land(1)
        s.add1()
        s.start(2)
    for s in sums:
        s.land(2)
        s.add2()
        s.start(3)
    for i, s in enumerate(sums):
        s.land(3)
        total = s.add3()
        if i < 2:
            out_q[16 * i : 16 * i + 16] = total[:, 0:384]
            out_t[16 * i : 16 * i + 16] = total[:, 384:512]
        else:
            out_s[...] = total
    for s in sums:
        s.gone()


def call(kernel, outs, scratch, collective_id=None):
    vmem = pl.BlockSpec(memory_space=pltpu.VMEM)
    params = dict(vmem_limit_bytes=VLIMIT)
    if collective_id is not None:
        params.update(collective_id=collective_id, has_side_effects=True)

    def run(*args):
        return pl.pallas_call(
            kernel,
            out_shape=[jax.ShapeDtypeStruct(s, t) for s, t in outs],
            in_specs=[vmem] * len(args),
            out_specs=[vmem] * len(outs),
            scratch_shapes=scratch,
            compiler_params=pltpu.CompilerParams(**params),
        )(*args)

    return run


def shards(
    stream,
    spatial_out,
    spatial_qkv,
    upstream,
    proj_spatial,
    qkv_temporal,
    proj_temporal,
    mod_weight,
    noise_steps,
    positions,
    memory,
):
    dma = pltpu.SemaphoreType.DMA
    embedding = frame_embedding(noise_steps, mod_weight.shape[0]).astype(BF16)
    gain = 1.0 + jnp.dot(embedding, mod_weight, preferred_element_type=F32)
    allowed = visible_frames(positions, memory)
    spread = jnp.repeat(jnp.repeat(allowed.T, SLOT, axis=0), SLOT, axis=1)
    slot = jnp.arange(ROWS, dtype=jnp.int32) % SLOT
    bias = jnp.where(jnp.logical_and(spread, slot[:, None] == slot[None, :]), 0.0, NEG).astype(F32)

    recv, recv_s = call(
        forward_kernel,
        [((NF, 16, D), BF16), ((NP, 3, PAD, 128), BF16)],
        [
            pltpu.VMEM((2, 128, D), F32),
            pltpu.VMEM((2, 128, D), F32),
            pltpu.VMEM((NF, 16, D), BF16),
            pltpu.VMEM((NP, 3, PAD, 128), BF16),
            dma((NF,)),
            dma((NF,)),
            dma((NP,)),
            dma((NP,)),
            dma((1,)),
        ],
        0,
    )(stream, upstream, gain, spatial_qkv)

    term_a, term_b, gn = call(
        temporal_kernel,
        [((16, 2, NP, 16, 512), BF16), ((16, 2, NP, 16, 512), BF16), ((NF, 16, 512), BF16)],
        [
            pltpu.VMEM((ROWS, D), BF16),
            pltpu.VMEM((ROWS, D), BF16),
            pltpu.VMEM((D, ROWS), BF16),
            pltpu.VMEM((ROWS, 3 * D), BF16),
            pltpu.VMEM((ROWS, D), BF16),
            pltpu.VMEM((ROWS, D), BF16),
            pltpu.VMEM((ROWS, 3 * D), BF16),
            pltpu.VMEM((D, ROWS), BF16),
        ],
    )(recv, qkv_temporal, proj_temporal, bias)

    grad_stream, recv_g, term_p = call(
        back_kernel,
        [((2, TOK, D), BF16), ((NP, PAD, 128), BF16), ((16, 2, NP, 16, 128), BF16)],
        [
            pltpu.VMEM((NF, 16, 512), BF16),
            pltpu.VMEM((2, PAD, D), F32),
            pltpu.VMEM((2, PAD, 512), BF16),
            pltpu.VMEM((NP, PAD, 128), BF16),
            dma((NF,)),
            dma((NF,)),
            dma((NP,)),
            dma((NP,)),
            dma((1,)),
        ],
        1,
    )(gn, stream, upstream, gain, proj_spatial, spatial_out)

    (grad_spatial_qkv,) = call(
        spatial_kernel,
        [((2, TOK, 1536), BF16)],
        [
            pltpu.VMEM((SP, 128), BF16),
            pltpu.VMEM((SP, 128), BF16),
            pltpu.VMEM((SP, 128), F32),
            pltpu.VMEM((SP, 128), F32),
            pltpu.VMEM((2, SP, 128), F32),
            pltpu.VMEM((NP, 3, PAD, 128), BF16),
            pltpu.VMEM((NP, 3, PAD, 128), BF16),
            dma((NP,)),
            dma((NP,)),
        ],
        2,
    )(recv_s, recv_g)

    grad_q, grad_t, grad_s = call(
        sum_kernel,
        [((32, 384), F32), ((32, 128), F32), ((16, 128), F32)],
        sum_scratch(512, True) + sum_scratch(512, False) + sum_scratch(128, True),
        3,
    )(term_a, term_b, term_p)
    return (grad_stream, grad_spatial_qkv, grad_s, grad_q, grad_t)


def solution(mesh):
    in_specs = (
        P("frame", "patch", None),
        P("frame", "patch", None),
        P("frame", "patch", None),
        P("frame", "patch", None),
        P(),
        P(),
        P(),
        P(),
        P("frame"),
        P(),
        P(),
    )
    out_specs = (
        P("frame", "patch", None),
        P("frame", "patch", None),
        P("frame", "patch"),
        P("frame", "patch"),
        P("frame", "patch"),
    )
    return jax.shard_map(shards, mesh=mesh, in_specs=in_specs, out_specs=out_specs, check_vma=False)
```

time: 718 us -> 200 us (0.28); the launches traced: 708 us -> 198 us
  waiting for transfers between devices: 423 us -> 0 us
  Pallas kernels: 0 us -> 177 us
  local copies, waits for them, and re-layouts: 98.4 us -> 16.1 us
  starting transfers between devices: 74.6 us -> 0 us
  matrix products: 71.7 us -> 0.78 us
  blocking collectives: 21.4 us -> 0 us
  between operations: 15.4 us -> 0.75 us
    reduce_scatter x3 -> x0, waiting for transfers between devices: 240 us -> none  [the longest x1 126 us: shards(): lax.psum_scatter(term_qkv_temporal.astype(jnp.bfloat16), 'frame', scatter...]
    pallas_call x0 -> x5, Pallas kernels: none -> 177 us  [run(): pl.pallas_call(kernel, out_shape=[jax.ShapeDtypeStruct(s, t) for s, t in...]
    all_to_all x14 -> x0, waiting for transfers between devices: 92.6 us -> none  [the longest x1 14 us: shards(): lax.all_to_all(to_pairs(projected[:, :, 0]), 'frame', split_axis=1, conca...]
    unnamed x9 -> x0, waiting for transfers between devices: 90.5 us -> none
    all_to_all x14 -> x0, starting transfers between devices: 74.3 us -> none  [the longest x1 11.6 us: shards(): lax.all_to_all(to_pairs(grad_out_t), 'frame', split_axis=1, concat_axis=0...]
    dot_general x17 -> x1, matrix products: 63.8 us -> 0.78 us  [shards(): gain = 1.0 + jnp.dot(embedding, mod_weight, preferred_element_type=F32)]
    unnamed x81 -> x13, local copies, waits for them, and re-layouts: 48.6 us -> 15.6 us
    all_to_all x1 -> x0, blocking collectives: 21.4 us -> none  [shards(): lax.all_to_all(frame_major(outcome[0]), 'frame', split_axis=0, concat_axi...]
  transfers between devices with their start and end apart: 20 -> 0, of which waited for: 18 -> 0; matrix products, arithmetic and copies ran while one was open for 19% -> 0% of each run, Pallas kernels for 0% -> 0%
where the time goes in v1:
time: 200 us; the launch traced here: 198 us
  Pallas kernels  177 us (88%)
  local copies, waits for them, and re-layouts  16.1 us (8%)
  other arithmetic  3.25 us (2%)
    pallas_call x5, Pallas kernels, run(): pl.pallas_call(kernel, out_shape=[jax.ShapeDtypeStruct(s, t) for s, t in...  177 us
    unnamed x13, local copies, waits for them, and re-layouts  15.6 us

profile of v1, /device:TPU:16, one launch (start us, length us, event | category | flops | bytes accessed | tf_op | source)
XLA Modules:
  0.0 198.2 jit_solution(4252342485286171722)
XLA Ops:
  0.6 0.0 copy-start
  0.6 0.7 convert_element_type.4
  1.4 0.1 fusion.1
  1.5 0.2 copy-done
  1.7 0.8 convolution_add_fusion.gain
  2.5 0.8 fusion
  3.3 0.8 bitcast_or_fusion
  4.1 0.1 copy.49
  4.2 0.1 copy.50
  4.3 0.1 broadcast_in_dim.11
  4.4 0.2 copy.51
  4.6 0.8 and_select_fusion.bias
  5.4 1.6 copy.54.so
  7.1 1.9 copy.46.stream
  9.0 1.9 copy.47.upstream
  10.9 2.0 %copy.48.sqkv = bf16[2,110,1536]{2,1,0:T(8,128)(2,1)} copy(bf16[2,110,1536]{2,0,1:T(2,128)(2,1)} %param.13) | data formatting | bytes 1351680 | tf_op args[2]
  12.9 33.0 %shard_map.146 = (bf16[32,16,1024]{2,1,0:T(8,128)(2,1)}, bf16[8,3,112,128]{3,2,1,0:T(8,128)(2,1)}) custom-call(bf16[2,110,1024]{2,1,0:T(8,128)(2,1)} %copy.46.stream, bf16[2,110,1024]{2,1,0:T(8,128)(2,1)} %copy.47.upstream, f32[2,1024]{1,0:T(2,128)} %convolution_add_fusion.gain, bf16[2,110,1536]{2,1,0:T(8,128)(2,1)} %copy.48.sqkv), custom_call_target="tpu_custom_call" | custom-call | tf_op jit(solution)/shard_map/pallas_call | solution.py:588
  46.0 26.8 %shard_map.147 = (bf16[16,2,8,16,512]{4,3,2,1,0:T(8,128)(2,1)}, bf16[16,2,8,16,512]{4,3,2,1,0:T(8,128)(2,1)}, bf16[32,16,512]{2,1,0:T(8,128)(2,1)}) custom-call(bf16[32,16,1024]{2,1,0:T(8,128)(2,1)} %get-tuple-element.16.recv, bf16[1024,3072]{1,0:T(8,128)(2,1)} %wqkv.1, bf16[1024,1024]{1,0:T(8,128)(2,1)} %wp.1, f32[256,256]{1,0:T(8,128)} %and_select_fusion.bias), custom_call_target="tpu_custom_call" | custom-call | tf_op jit(solution)/shard_map/pallas_call | solution.py:588
  72.7 37.4 %shard_map.148 = (bf16[2,110,1024]{2,1,0:T(8,128)(2,1)}, bf16[8,112,128]{2,1,0:T(8,128)(2,1)}, bf16[16,2,8,16,128]{4,3,2,1,0:T(8,128)(2,1)}) custom-call(bf16[32,16,512]{2,1,0:T(8,128)(2,1)} %get-tuple-element.17.gn, bf16[2,110,1024]{2,1,0:T(8,128)(2,1)} %copy.46.stream, bf16[2,110,1024]{2,1,0:T(8,128)(2,1)} %copy.47.upstream, ...), custom_call_target="tpu_custom_call" | custom-call | tf_op jit(solution)/shard_map/pallas_call | solution.py:588
  110.2 0.0 copy-start.1
  110.2 56.7 %shard_map.150 = (f32[32,384]{1,0:T(8,128)}, f32[32,128]{1,0:T(8,128)}, f32[16,128]{1,0:T(8,128)}) custom-call(bf16[16,2,8,16,512]{4,3,2,1,0:T(8,128)(2,1)} %get-tuple-element.21.term_a, bf16[16,2,8,16,512]{4,3,2,1,0:T(8,128)(2,1)} %get-tuple-element.22.term_b, bf16[16,2,8,16,128]{4,3,2,1,0:T(8,128)(2,1)} %get-tuple-element.23.term_p), custom_call_target="tpu_custom_call" | custom-call | tf_op jit(solution)/shard_map/pallas_call | solution.py:588
  166.9 0.0 copy-done.1
  166.9 1.2 copy.55
  168.1 23.4 %shard_map.149 = bf16[2,110,1536]{2,1,0:T(8,128)(2,1)} custom-call(bf16[8,3,112,128]{3,2,1,0:T(8,128)(2,1)} %get-tuple-element.19.qkv, bf16[8,112,128]{2,1,0:T(8,128)(2,1)} %get-tuple-element.20.gg), custom_call_target="tpu_custom_call" | custom-call | tf_op jit(solution)/shard_map/pallas_call | solution.py:588
  191.5 2.6 %copy.56 = bf16[2,110,1536]{2,0,1:T(2,128)(2,1)} copy(bf16[2,110,1536]{2,1,0:T(8,128)(2,1)} %shard_map.149) | data formatting | bytes 1351680
  194.2 1.3 copy.60
  195.5 1.4 copy.61
  196.9 1.3 copy.62
  (4 shorter events, 0.1 us)
Async XLA Ops:
  0.6 1.1 copy-start
  110.2 56.7 %copy-start.1 = (bf16[2,110,1024]{2,1,0:T(8,128)(2,1)S(1)}, bf16[2,110,1024]{2,1,0:T(8,128)(2,1)}, u32[]{:S(2)}) copy-start(bf16[2,110,1024]{2,1,0:T(8,128)(2,1)} %get-tuple-element.42) | copy-start | bytes 1351684

commit v2 on v0

v2 whole, which is shorter than its diff:
```python
import functools

import jax
import jax.numpy as jnp
from jax import lax
from jax.experimental import pallas as pl
from jax.experimental.pallas import tpu as pltpu
from jax.sharding import PartitionSpec as P

MESH = pl.DeviceIdType.MESH
F32 = jnp.float32
BF16 = jnp.bfloat16
D = 1024
E = 64
F = 64
NF = 32
NP = 8
TOK = 110
PAD = 112
SLOT = 4
BUSY = 28
ROWS = F * SLOT
SP = NP * PAD
SCALE = E ** (-0.5)
NEG = -1e30
VLIMIT = 61 * 1024 * 1024


def frame_embedding(noise_steps, embed_width):
    half_width = embed_width // 2
    counter = jnp.arange(half_width, dtype=jnp.float32)
    frequency = jnp.exp(-jnp.log(10000.0) * counter / half_width)
    angles = noise_steps.astype(jnp.float32)[:, None] * frequency[None, :]
    return jnp.concatenate([jnp.cos(angles), jnp.sin(angles)], axis=1)


def visible_frames(positions, memory):
    frame_total = positions.shape[0]
    earlier = positions[None, :] <= positions[:, None]
    frame_ids = jnp.arange(frame_total, dtype=jnp.int32)
    recalled = jnp.any(memory[:, :, None] == frame_ids[None, None, :], axis=1)
    return jnp.logical_or(earlier, recalled)


def rcopy(src, dst, ssem, rsem, f, p):
    return pltpu.make_async_remote_copy(
        src_ref=src, dst_ref=dst, send_sem=ssem, recv_sem=rsem, device_id=(f, p), device_id_type=MESH
    )


def low_rows():
    return lax.broadcasted_iota(jnp.int32, (8, D), 0) < 4


def swap_halves(a, b, low):
    return jnp.where(low, a, pltpu.roll(b, 4, 0)), jnp.where(low, pltpu.roll(a, 4, 0), b)


def swap_lanes(a, b):
    low = lax.broadcasted_iota(jnp.int32, a.shape, 1) < E
    return jnp.where(low, a, pltpu.roll(b, E, 1)), jnp.where(low, pltpu.roll(a, E, 1), b)


def dot(a, b, da, db):
    return lax.dot_general(a, b, (((da,), (db,)), ((), ())), preferred_element_type=F32)


def place():
    me_f, me_p = lax.axis_index("frame"), lax.axis_index("patch")
    z, y_hi, core = me_f // 4, lax.rem(me_f // 2, 2), lax.rem(me_f, 2)
    x, y_lo = me_p // 2, lax.rem(me_p, 2)
    return z, y_hi, core, x, y_lo


def device(z, y, core, x):
    return z * 4 + (y // 2) * 2 + core, x * 2 + lax.rem(y, 2)


def barrier():
    me_f, me_p = lax.axis_index("frame"), lax.axis_index("patch")
    z, y_hi, core, x, y_lo = place()
    y = y_hi * 2 + y_lo
    sem = pltpu.get_barrier_semaphore()

    def greet(f, p):
        pl.semaphore_signal(sem, inc=1, device_id=(f, p), device_id_type=MESH)

    def frames(k, _):
        greet(lax.rem(me_f + k, NF), me_p)
        return 0

    lax.fori_loop(1, NF, frames, 0)

    def patches(k, _):
        greet(me_f, lax.rem(me_p + k, NP))
        return 0

    lax.fori_loop(1, NP, patches, 0)
    greet(*device(z, lax.rem(y + 1, 4), core, x))
    greet(*device(z, lax.rem(y + 3, 4), core, x))
    pl.semaphore_wait(sem, NF + NP)


class Exchange:
    def __init__(self, src, dst, sems, along_frame, sends=None, takes=None):
        self.src, self.dst, (self.ssem, self.rsem) = src, dst, sems
        self.along_frame, self.sends, self.takes = along_frame, sends, takes
        self.me_f, self.me_p = lax.axis_index("frame"), lax.axis_index("patch")
        self.n = NF if along_frame else NP
        self.me = self.me_f if along_frame else self.me_p

    def copy(self, k):
        to = lax.rem(self.me + k, self.n)
        where = (to, self.me_p) if self.along_frame else (self.me_f, to)
        return rcopy(self.src.at[to], self.dst.at[self.me], self.ssem.at[k], self.rsem.at[k], *where)

    def each(self, act, wanted):
        def body(k, _):
            if wanted is None:
                act(self.copy(k))
            else:

                @pl.when(wanted(k))
                def _():
                    act(self.copy(k))

            return 0

        lax.fori_loop(1, self.n, body, 0)

    def start(self):
        self.each(lambda c: c.start(), self.sends)

    def land(self):
        self.each(lambda c: c.wait_recv(), self.takes)

    def gone(self):
        self.each(lambda c: c.wait_send(), self.sends)


class Sum:
    def __init__(self, term, bufs, x_first):
        self.term, self.x_first = term, x_first
        (self.r0, self.t2, self.t3, self.in1, self.up1, self.full1, self.in2, self.up2, self.full2, self.r3,
         self.ssem, self.rsem) = bufs
        self.z, self.y_hi, self.core, self.x, self.y_lo = place()
        self.y = self.y_hi * 2 + self.y_lo
        self.cols = term.shape[-1]

    def chunk(self, stage, j):
        if stage == 1:
            if self.x_first:
                return self.term.at[:, :, self.core, j]
            return self.term.at[:, j // 2, self.core, :, lax.rem(j, 2)]
        if self.x_first:
            return self.t2.at[:, j // 2, lax.rem(j, 2)]
        return self.t2.at[:, j]

    def ring(self, stage):
        if (stage == 1) == self.x_first:
            return self.x, lambda j: device(self.z, self.y, self.core, j)
        return self.y, lambda j: device(self.z, j, self.core, self.x)

    def core_copy(self, x, y_lo):
        other = 1 - self.core
        s = x * 2 + y_lo
        return rcopy(
            self.term.at[:, :, other, x, y_lo], self.r0.at[:, :, x, y_lo], self.ssem.at[s], self.rsem.at[s],
            *device(self.z, self.y, other, self.x),
        )

    def core_add(self, x, y_lo):
        self.core_copy(x, y_lo).wait_recv()

        def body(z, _):
            mine = self.term[z, :, self.core, x, y_lo].astype(F32)
            self.term[z, :, self.core, x, y_lo] = (mine + self.r0[z, :, x, y_lo].astype(F32)).astype(BF16)
            return 0

        lax.fori_loop(0, 8, body, 0)

    def first(self, stage):
        me, at = self.ring(stage)
        far = lax.rem(me + 2, 4)
        into = self.in1 if stage == 1 else self.in2
        s = 8 if stage == 1 else 12
        return [
            rcopy(
                self.chunk(stage, far).at[4 * h : 4 * h + 4], into.at[h], self.ssem.at[s + h], self.rsem.at[s + h],
                *at(lax.rem(me + (1, 3)[h], 4)),
            )
            for h in range(2)
        ]

    def second(self, stage):
        me, at = self.ring(stage)
        up = self.up1 if stage == 1 else self.up2
        full = self.full1 if stage == 1 else self.full2
        s = 10 if stage == 1 else 14
        return [
            rcopy(up.at[h], full.at[h], self.ssem.at[s + h], self.rsem.at[s + h], *at(lax.rem(me + (1, 3)[h], 4)))
            for h in range(2)
        ]

    def relay(self, stage):
        me, _ = self.ring(stage)
        into = self.in1 if stage == 1 else self.in2
        up = self.up1 if stage == 1 else self.up2
        firsts, seconds = self.first(stage), self.second(stage)
        for h in range(2):
            mine = self.chunk(stage, lax.rem(me + (1, 3)[h], 4))
            firsts[h].wait_recv()

            def body(z, _):
                a = 4 * h + z
                b = 4 * (1 - h) + z
                up[h, a] = (mine[a].astype(F32) + into[h, z].astype(F32)).astype(BF16)
                up[h, b] = mine[b]
                return 0

            lax.fori_loop(0, 4, body, 0)
            seconds[h].start()

    def ring_add(self, stage):
        me, _ = self.ring(stage)
        full = self.full1 if stage == 1 else self.full2
        out = self.t2 if stage == 1 else self.t3
        mine = self.chunk(stage, me)
        for c in self.second(stage):
            c.wait_recv()

        def body(z, _):
            total = mine[z].astype(F32) + full[0, z].astype(F32) + full[1, z].astype(F32)
            out[z] = total.astype(BF16)
            return 0

        lax.fori_loop(0, 8, body, 0)

    def last(self):
        out = []
        for k in range(1, 8):
            to = lax.rem(self.z + k, 8)
            out.append(
                rcopy(
                    self.t3.at[to], self.r3.at[k - 1], self.ssem.at[15 + k], self.rsem.at[15 + k],
                    *device(to, self.y, self.core, self.x),
                )
            )
        return out

    def total(self):
        total = self.t3[self.z].astype(F32)
        for c in self.last():
            c.wait_recv()
        for k in range(7):
            total = total + self.r3[k].astype(F32)
        return total

    def start(self, copies):
        for c in copies:
            c.start()

    def gone(self):
        for x in range(4):
            for y_lo in range(2):
                self.core_copy(x, y_lo).wait_send()
        for c in self.first(1) + self.second(1) + self.first(2) + self.second(2) + self.last():
            c.wait_send()


def sum_scratch(cols, x_first):
    mid = (2, 2) if x_first else (4,)
    tile = (16, cols)
    return [
        pltpu.VMEM((8, 2, 4, 2) + tile, BF16),
        pltpu.VMEM((8,) + mid + tile, BF16),
        pltpu.VMEM((8,) + tile, BF16),
        pltpu.VMEM((2, 4) + mid + tile, BF16),
        pltpu.VMEM((2, 8) + mid + tile, BF16),
        pltpu.VMEM((2, 8) + mid + tile, BF16),
        pltpu.VMEM((2, 4) + tile, BF16),
        pltpu.VMEM((2, 8) + tile, BF16),
        pltpu.VMEM((2, 8) + tile, BF16),
        pltpu.VMEM((7,) + tile, BF16),
        pltpu.SemaphoreType.DMA((23,)),
        pltpu.SemaphoreType.DMA((23,)),
    ]


NSUM = 12


def whole_kernel(
    stream, upstream, so, sqkv, gain, pos, memo, wqkv_hbm, wp_hbm, wps_hbm,
    gs_out, out, out_q, out_t, out_s,
    wqkv, wp, wps, wsem,
    nbuf, ubuf, send, recv, ssem, rsem, lsem,
    send_s, recv_s, ssem_s, rsem_s,
    bias, nv, uv, nt, proj, g, o, dqkv, ot,
    gn, recv_gn, ssem_n, rsem_n,
    sopad, send_g, recv_g, ssem_g, rsem_g,
    kq, probs, send_b, recv_b, ssem_b, rsem_b,
    term_a, term_b, term_p, *sum_bufs,
):
    me_f, me_p = lax.axis_index("frame"), lax.axis_index("patch")
    owner = me_f < BUSY
    loads = [
        pltpu.make_async_copy(wqkv_hbm, wqkv, wsem.at[0]),
        pltpu.make_async_copy(wp_hbm, wp, wsem.at[1]),
        pltpu.make_async_copy(wps_hbm, wps, wsem.at[2]),
    ]
    for c in loads:
        c.start()
    sums = [
        Sum(term, sum_bufs[NSUM * i : NSUM * i + NSUM], x_first)
        for i, (term, x_first) in enumerate(((term_a, True), (term_b, False), (term_p, True)))
    ]
    sum_a, sum_b, sum_p = sums

    for f in range(2):
        x = stream[f].astype(F32)
        inverse = lax.rsqrt(jnp.mean(x * x, axis=-1, keepdims=True) + 1e-06)
        nbuf[f, 104:PAD] = jnp.zeros((8, D), F32)
        ubuf[f, 104:PAD] = jnp.zeros((8, D), F32)
        nbuf[f, 0:TOK] = x * inverse * gain[f : f + 1]
        ubuf[f, 0:TOK] = upstream[f].astype(F32)

    low8 = low_rows()

    def pack(i, _):
        rows = pl.ds(pl.multiple_of(i * 8, 8), 8)
        n0, n1 = swap_halves(nbuf[0, rows], nbuf[1, rows], low8)
        u0, u1 = swap_halves(ubuf[0, rows], ubuf[1, rows], low8)
        send[2 * i] = jnp.concatenate([n0, u0], axis=0).astype(BF16)
        send[2 * i + 1] = jnp.concatenate([n1, u1], axis=0).astype(BF16)
        return 0

    lax.fori_loop(0, BUSY // 2, pack, 0)

    @pl.when(jnp.logical_not(owner))
    def _():
        recv[...] = jnp.zeros(recv.shape, BF16)

    barrier()
    out_x = Exchange(
        send, recv, (ssem, rsem), True, lambda k: lax.rem(me_f + k, NF) < BUSY, lambda k: owner
    )
    out_x.start()
    local = pltpu.make_async_copy(send.at[me_f], recv.at[me_f], lsem.at[0])

    @pl.when(owner)
    def _():
        local.start()

    send_s[:, :, 96:PAD] = jnp.zeros((NP, 3, 16, 128), BF16)
    for j in range(4):
        v = []
        for f in range(2):
            a = sqkv[f, :, 128 * j : 128 * j + 128].astype(F32)
            b = sqkv[f, :, 512 + 128 * j : 640 + 128 * j].astype(F32)
            m0, m1 = swap_lanes(a, b)
            send_s[2 * j, f, 0:TOK] = m0.astype(BF16)
            send_s[2 * j + 1, f, 0:TOK] = m1.astype(BF16)
            v.append(sqkv[f, :, 1024 + 128 * j : 1152 + 128 * j].astype(F32))
        m0, m1 = swap_lanes(v[0], v[1])
        send_s[2 * j, 2, 0:TOK] = m0.astype(BF16)
        send_s[2 * j + 1, 2, 0:TOK] = m1.astype(BF16)
    head_x = Exchange(send_s, recv_s, (ssem_s, rsem_s), False)
    head_x.start()
    recv_s[me_p] = send_s[me_p]
    for f in range(2):
        sopad[f, 96:PAD] = jnp.zeros((16, 512), BF16)
        sopad[f, 0:TOK] = so[f]

    def frame_of(i):
        return (i // 8) * 2 + lax.rem(i, 8) // 4

    table = jnp.concatenate(
        [pos[...].astype(F32), memo[...].astype(F32), jnp.zeros((3, F), F32)], axis=0
    ).astype(BF16)
    at_col = (
        lax.broadcasted_iota(jnp.int32, (F, ROWS), 0) == frame_of(lax.broadcasted_iota(jnp.int32, (F, ROWS), 1))
    )
    at_row = (
        lax.broadcasted_iota(jnp.int32, (ROWS, F), 1) == frame_of(lax.broadcasted_iota(jnp.int32, (ROWS, F), 0))
    )
    asked = dot(table, jnp.where(at_col, 1.0, 0.0).astype(BF16), 1, 0)
    held = dot(jnp.where(at_row, 1.0, 0.0).astype(BF16), table, 1, 1)
    key = lax.broadcasted_iota(jnp.int32, (ROWS, ROWS), 0)
    key_frame = frame_of(key).astype(F32)
    seen = held[:, 0:1] <= asked[0:1]
    for m in range(4):
        seen = jnp.logical_or(seen, key_frame == asked[1 + m : 2 + m])
    same = lax.rem(key, SLOT) == lax.rem(lax.broadcasted_iota(jnp.int32, (ROWS, ROWS), 1), SLOT)
    bias[...] = jnp.where(jnp.logical_and(seen, same), 0.0, NEG).astype(F32)

    head_x.land()
    low = lax.broadcasted_iota(jnp.int32, (SP, 128), 1) < E
    dead = lax.rem(lax.broadcasted_iota(jnp.int32, (SP, 128), 0), PAD) >= TOK
    dead_bias = jnp.where(dead, NEG, 0.0).astype(F32)
    for f in range(2):
        x = recv_s[:, f].reshape(SP, 128).astype(F32)
        kq[...] = jnp.where(low, pltpu.roll(x, E, 1), 0.0).astype(BF16)
        for b in range(SP // 128):
            rows = slice(b * 128, b * 128 + 128)
            st = dot(kq[...], x[rows].astype(BF16), 1, 1) * SCALE + dead_bias
            e = jnp.exp(st - jnp.max(st, axis=0, keepdims=True))
            probs[f, :, rows] = (e / jnp.sum(e, axis=0, keepdims=True)).astype(BF16)

    out_x.land()

    @pl.when(owner)
    def _():
        local.wait()

    for c in loads:
        c.wait()
    x = recv[...].astype(F32)
    nv[...] = x[:, 0:8].reshape(ROWS, D).astype(BF16)
    uv[...] = x[:, 8:16].reshape(ROWS, D).astype(BF16)
    nt[...] = nv[...].T

    def project(c, _):
        cols = pl.ds(pl.multiple_of(c * 512, 512), 512)
        proj[:, cols] = dot(nv[...], wqkv[:, cols], 1, 0).astype(BF16)
        return 0

    lax.fori_loop(0, 6, project, 0)

    def project_g(c, _):
        cols = pl.ds(pl.multiple_of(c * 512, 512), 512)
        g[:, cols] = dot(uv[...], wp[cols, :], 1, 1).astype(BF16)
        return 0

    lax.fori_loop(0, 2, project_g, 0)
    low_t = lax.broadcasted_iota(jnp.int32, (ROWS, 128), 1) < E

    def pair(j, _):
        def cols(base):
            return pl.ds(pl.multiple_of(base + j * 128, 128), 128)

        qp, kp, vp, gp = proj[:, cols(0)], proj[:, cols(D)], proj[:, cols(2 * D)], g[:, cols(0)]
        parts = []
        for half in range(2):
            mine = low_t if half == 0 else jnp.logical_not(low_t)
            zero = jnp.zeros_like(qp)
            kh = jnp.where(mine, kp, zero)
            vh = jnp.where(mine, vp, zero)
            st = dot(kh, qp, 1, 1) * SCALE + bias[...]
            e = jnp.exp(st - jnp.max(st, axis=0, keepdims=True))
            p = e / jnp.sum(e, axis=0, keepdims=True)
            pb = p.astype(BF16)
            dp = dot(vh, gp, 1, 1)
            ds = (p * (dp - jnp.sum(p * dp, axis=0, keepdims=True)) * SCALE).astype(BF16)
            parts.append(
                (dot(pb, vp, 0, 0), dot(ds, kp, 0, 0), dot(ds, qp, 1, 0), dot(pb, gp, 1, 0))
            )
        res = [jnp.where(low_t, a, b).astype(BF16) for a, b in zip(*parts)]
        o[:, cols(0)] = res[0]
        dqkv[:, cols(0)] = res[1]
        dqkv[:, cols(D)] = res[2]
        dqkv[:, cols(2 * D)] = res[3]
        return 0

    lax.fori_loop(0, 8, pair, 0)
    back = dot(dqkv[...], wqkv[...], 1, 1).reshape(NF, 8, D)
    gn[...] = jnp.concatenate([back[:, :, 0:512], back[:, :, 512:1024]], axis=1).astype(BF16)

    back_x = Exchange(
        gn, recv_gn, (ssem_n, rsem_n), True, lambda k: owner, lambda k: lax.rem(me_f + NF - k, NF) < BUSY
    )
    back_x.start()
    local_n = pltpu.make_async_copy(gn.at[me_f], recv_gn.at[me_f], lsem.at[1])

    @pl.when(owner)
    def _():
        local_n.start()

    ot[...] = o[...].T

    def weights(p, _):
        x, y_lo = p // 2, lax.rem(p, 2)
        r = dot(nt[...], dqkv[:, pl.ds(pl.multiple_of(p * 384, 128), 384)], 1, 0)
        r = r.reshape(8, 2, 2, 32, 384)
        s = dot(ot[...], uv[:, pl.ds(pl.multiple_of(p * 128, 128), 128)], 1, 0)
        s = s.reshape(8, 2, 2, 32, 128)
        term_a[:, :, :, x, y_lo, :, 0:384] = r[:, :, :, 0:16].astype(BF16)
        term_a[:, :, :, x, y_lo, :, 384:512] = s[:, :, :, 0:16].astype(BF16)
        sum_a.core_copy(x, y_lo).start()
        term_b[:, :, :, x, y_lo, :, 0:384] = r[:, :, :, 16:32].astype(BF16)
        term_b[:, :, :, x, y_lo, :, 384:512] = s[:, :, :, 16:32].astype(BF16)
        sum_b.core_copy(x, y_lo).start()
        return 0

    lax.fori_loop(0, NP, weights, 0)

    def cores(p, _):
        x, y_lo = p // 2, lax.rem(p, 2)
        sum_a.core_add(x, y_lo)
        sum_b.core_add(x, y_lo)
        return 0

    lax.fori_loop(0, NP, cores, 0)
    for s in (sum_a, sum_b):
        s.start(s.first(1))

    back_x.land()

    @pl.when(owner)
    def _():
        local_n.wait()

    def unpack(i, _):
        rows = pl.ds(pl.multiple_of(i * 8, 8), 8)
        x = recv_gn[2 * i].astype(F32)
        y = recv_gn[2 * i + 1].astype(F32)
        x = jnp.concatenate([x[0:8], x[8:16]], axis=1)
        y = jnp.concatenate([y[0:8], y[8:16]], axis=1)
        nbuf[0, rows], nbuf[1, rows] = swap_halves(x, y, low8)
        return 0

    lax.fori_loop(0, BUSY // 2, unpack, 0)
    for f in range(2):
        x = stream[f].astype(F32)
        inverse = lax.rsqrt(jnp.mean(x * x, axis=-1, keepdims=True) + 1e-06)
        scaled = nbuf[f, 0:TOK] * gain[f : f + 1]
        inner = jnp.mean(x * scaled, axis=-1, keepdims=True)
        res = upstream[f].astype(F32) + inverse * scaled - x * (inverse * inverse * inverse) * inner
        gs_out[f] = res.astype(BF16)
        nbuf[f, 104:PAD] = jnp.zeros((8, D), F32)
        nbuf[f, 0:TOK] = res
    gs = nbuf[...].reshape(2 * PAD, D).astype(BF16)
    gos = dot(gs, wps[...], 1, 1)
    for j in range(4):
        cols = slice(128 * j, 128 * j + 128)
        m0, m1 = swap_lanes(gos[0:PAD, cols], gos[PAD : 2 * PAD, cols])
        send_g[2 * j] = m0.astype(BF16)
        send_g[2 * j + 1] = m1.astype(BF16)
    cot_x = Exchange(send_g, recv_g, (ssem_g, rsem_g), False)
    cot_x.start()
    recv_g[me_p] = send_g[me_p]
    tp = dot(sopad[...].reshape(2 * PAD, 512), gs, 0, 0)
    for p in range(NP):
        term_p[:, :, :, p // 2, p % 2] = tp[:, 128 * p : 128 * p + 128].reshape(8, 2, 2, 16, 128).astype(BF16)
        sum_p.core_copy(p // 2, p % 2).start()
    for s in (sum_a, sum_b):
        s.relay(1)
    for p in range(NP):
        sum_p.core_add(p // 2, p % 2)
    sum_p.start(sum_p.first(1))

    cot_x.land()
    g_all = recv_g[...].reshape(SP, 128)
    v_all = recv_s[:, 2].reshape(SP, 128).astype(F32)
    dvs = []
    for f in range(2):
        dvs.append(dot(probs[f], g_all, 1, 0))
        qk = recv_s[:, f].reshape(SP, 128)
        kq[...] = jnp.where(low if f == 0 else jnp.logical_not(low), v_all, 0.0).astype(BF16)
        for b in range(SP // 128):
            rows = slice(b * 128, b * 128 + 128)
            p = probs[f, :, rows].astype(F32)
            dp = dot(kq[...], g_all[rows], 1, 1)
            ds = p * (dp - jnp.sum(p * dp, axis=0, keepdims=True)) * SCALE
            probs[f, :, rows] = ds.astype(BF16)
        dk = dot(probs[f], qk, 1, 0)
        dq = dot(probs[f], qk, 0, 0)
        send_b[:, f] = jnp.where(low, dk, dq).astype(BF16).reshape(NP, PAD, 128)
        if f == 0:
            for s in (sum_a, sum_b):
                s.ring_add(1)
                s.start(s.first(2))
            sum_p.relay(1)
    send_b[:, 2] = jnp.where(low, dvs[0], dvs[1]).astype(BF16).reshape(NP, PAD, 128)
    token_x = Exchange(send_b, recv_b, (ssem_b, rsem_b), False)
    token_x.start()
    recv_b[me_p] = send_b[me_p]
    for s in (sum_a, sum_b):
        s.relay(2)
    sum_p.ring_add(1)
    sum_p.start(sum_p.first(2))
    for s in (sum_a, sum_b):
        s.ring_add(2)
        s.start(s.last())
    sum_p.relay(2)
    sum_p.ring_add(2)
    sum_p.start(sum_p.last())

    token_x.land()
    for j in range(4):
        c = 128 * j
        for f in range(2):
            k, q = swap_lanes(recv_b[2 * j, f].astype(F32), recv_b[2 * j + 1, f].astype(F32))
            out[f, :, c : c + 128] = q[0:TOK].astype(BF16)
            out[f, :, 512 + c : 640 + c] = k[0:TOK].astype(BF16)
        v0, v1 = swap_lanes(recv_b[2 * j, 2].astype(F32), recv_b[2 * j + 1, 2].astype(F32))
        out[0, :, 1024 + c : 1152 + c] = v0[0:TOK].astype(BF16)
        out[1, :, 1024 + c : 1152 + c] = v1[0:TOK].astype(BF16)
    for i, s in enumerate((sum_a, sum_b)):
        total = s.total()
        out_q[16 * i : 16 * i + 16] = total[:, 0:384]
        out_t[16 * i : 16 * i + 16] = total[:, 384:512]
    out_s[...] = sum_p.total()
    out_x.gone()
    head_x.gone()
    back_x.gone()
    cot_x.gone()
    token_x.gone()
    for s in sums:
        s.gone()


def hand_over(q, t, s, out_q, out_t, out_s):
    out_q[...] = q[...]
    out_t[...] = t[...]
    out_s[...] = s[...]


def shards(
    stream,
    spatial_out,
    spatial_qkv,
    upstream,
    proj_spatial,
    qkv_temporal,
    proj_temporal,
    mod_weight,
    noise_steps,
    positions,
    memory,
):
    embedding = frame_embedding(noise_steps, mod_weight.shape[0]).astype(BF16)
    gain = 1.0 + jnp.dot(embedding, mod_weight, preferred_element_type=F32)
    vmem = pl.BlockSpec(memory_space=pltpu.VMEM)
    hbm = pl.BlockSpec(memory_space=pl.ANY)

    def pair_of(n):
        return [pltpu.SemaphoreType.DMA((n,)), pltpu.SemaphoreType.DMA((n,))]

    small = [((32, 384), F32), ((32, 128), F32), ((16, 128), F32)]
    outs = [((2, TOK, D), BF16), ((2, TOK, 1536), BF16)] + small
    scratch = (
        [
            pltpu.VMEM((D, 3 * D), BF16),
            pltpu.VMEM((D, D), BF16),
            pltpu.VMEM((512, D), BF16),
            pltpu.SemaphoreType.DMA((3,)),
            pltpu.VMEM((2, PAD, D), F32),
            pltpu.VMEM((2, PAD, D), F32),
            pltpu.VMEM((NF, 16, D), BF16),
            pltpu.VMEM((NF, 16, D), BF16),
        ]
        + pair_of(NF)
        + [
            pltpu.SemaphoreType.DMA((2,)),
            pltpu.VMEM((NP, 3, PAD, 128), BF16),
            pltpu.VMEM((NP, 3, PAD, 128), BF16),
        ]
        + pair_of(NP)
        + [
            pltpu.VMEM((ROWS, ROWS), F32),
            pltpu.VMEM((ROWS, D), BF16),
            pltpu.VMEM((ROWS, D), BF16),
            pltpu.VMEM((D, ROWS), BF16),
            pltpu.VMEM((ROWS, 3 * D), BF16),
            pltpu.VMEM((ROWS, D), BF16),
            pltpu.VMEM((ROWS, D), BF16),
            pltpu.VMEM((ROWS, 3 * D), BF16),
            pltpu.VMEM((D, ROWS), BF16),
            pltpu.VMEM((NF, 16, 512), BF16),
            pltpu.VMEM((NF, 16, 512), BF16),
        ]
        + pair_of(NF)
        + [
            pltpu.VMEM((2, PAD, 512), BF16),
            pltpu.VMEM((NP, PAD, 128), BF16),
            pltpu.VMEM((NP, PAD, 128), BF16),
        ]
        + pair_of(NP)
        + [
            pltpu.VMEM((SP, 128), BF16),
            pltpu.VMEM((2, SP, SP), BF16),
            pltpu.VMEM((NP, 3, PAD, 128), BF16),
            pltpu.VMEM((NP, 3, PAD, 128), BF16),
        ]
        + pair_of(NP)
        + [
            pltpu.VMEM((8, 2, 2, 4, 2, 16, 512), BF16),
            pltpu.VMEM((8, 2, 2, 4, 2, 16, 512), BF16),
            pltpu.VMEM((8, 2, 2, 4, 2, 16, 128), BF16),
        ]
        + sum_scratch(512, True)
        + sum_scratch(512, False)
        + sum_scratch(128, True)
    )
    grad_stream, grad_spatial_qkv, *totals = pl.pallas_call(
        whole_kernel,
        out_shape=[jax.ShapeDtypeStruct(s, t) for s, t in outs],
        in_specs=[vmem] * 7 + [hbm] * 3,
        out_specs=[vmem] * 5,
        scratch_shapes=scratch,
        compiler_params=pltpu.CompilerParams(vmem_limit_bytes=VLIMIT, collective_id=0, has_side_effects=True),
    )(
        stream,
        upstream,
        spatial_out,
        spatial_qkv,
        gain,
        positions.reshape(1, F),
        memory.T,
        qkv_temporal,
        proj_temporal,
        proj_spatial,
    )
    grad_q, grad_t, grad_s = pl.pallas_call(
        hand_over,
        out_shape=[jax.ShapeDtypeStruct(s, t) for s, t in small],
        in_specs=[vmem] * 3,
        out_specs=[vmem] * 3,
    )(*totals)
    return (grad_stream, grad_spatial_qkv, grad_s, grad_q, grad_t)


def solution(mesh):
    in_specs = (
        P("frame", "patch", None),
        P("frame", "patch", None),
        P("frame", "patch", None),
        P("frame", "patch", None),
        P(),
        P(),
        P(),
        P(),
        P("frame"),
        P(),
        P(),
    )
    out_specs = (
        P("frame", "patch", None),
        P("frame", "patch", None),
        P("frame", "patch"),
        P("frame", "patch"),
        P("frame", "patch"),
    )
    return jax.shard_map(shards, mesh=mesh, in_specs=in_specs, out_specs=out_specs, check_vma=False)
```

time: 718 us -> 134 us (0.19); the launches traced: 708 us -> 133 us
  waiting for transfers between devices: 423 us -> 0 us
  Pallas kernels: 0 us -> 118 us
  local copies, waits for them, and re-layouts: 98.4 us -> 12.5 us
  starting transfers between devices: 74.6 us -> 0 us
  matrix products: 71.7 us -> 0.78 us
  blocking collectives: 21.4 us -> 0 us
  between operations: 15.4 us -> 0.66 us
    reduce_scatter x3 -> x0, waiting for transfers between devices: 240 us -> none  [the longest x1 126 us: shards(): lax.psum_scatter(term_qkv_temporal.astype(jnp.bfloat16), 'frame', scatter...]
    pallas_call x0 -> x2, Pallas kernels: none -> 118 us  [the longest x1 117 us: shards(): pl.pallas_call(whole_kernel, out_shape=[jax.ShapeDtypeStruct(s, t) for s,...]
    all_to_all x14 -> x0, waiting for transfers between devices: 92.6 us -> none  [the longest x1 14 us: shards(): lax.all_to_all(to_pairs(projected[:, :, 0]), 'frame', split_axis=1, conca...]
    unnamed x9 -> x0, waiting for transfers between devices: 90.5 us -> none
    all_to_all x14 -> x0, starting transfers between devices: 74.3 us -> none  [the longest x1 11.6 us: shards(): lax.all_to_all(to_pairs(grad_out_t), 'frame', split_axis=1, concat_axis=0...]
    dot_general x17 -> x1, matrix products: 63.8 us -> 0.78 us  [shards(): gain = 1.0 + jnp.dot(embedding, mod_weight, preferred_element_type=F32)]
    unnamed x81 -> x8, local copies, waits for them, and re-layouts: 48.6 us -> 12.5 us
    all_to_all x1 -> x0, blocking collectives: 21.4 us -> none  [shards(): lax.all_to_all(frame_major(outcome[0]), 'frame', split_axis=0, concat_axi...]
  transfers between devices with their start and end apart: 20 -> 0, of which waited for: 18 -> 0; matrix products, arithmetic and copies ran while one was open for 19% -> 0% of each run, Pallas kernels for 0% -> 0%
where the time goes in v2:
time: 134 us; the launch traced here: 133 us
  Pallas kernels  118 us (88%)
  local copies, waits for them, and re-layouts  12.5 us (9%)
    pallas_call x1, Pallas kernels, shards(): pl.pallas_call(whole_kernel, out_shape=[jax.ShapeDtypeStruct(s, t) for s,...  117 us
    unnamed x8, local copies, waits for them, and re-layouts  12.5 us

profile of v2, /device:TPU:16, one launch (start us, length us, event | category | flops | bytes accessed | tf_op | source)
XLA Modules:
  0.0 133.2 jit_solution(4678005840814697810)
XLA Ops:
  0.6 0.0 copy-start
  0.6 0.7 convert_element_type.4
  1.4 0.1 fusion
  1.5 0.2 copy-done
  1.7 0.8 convolution_add_fusion.gain
  2.5 1.6 %copy.18.so = bf16[2,110,512]{2,1,0:T(8,128)(2,1)} copy(bf16[2,110,512]{2,0,1:T(2,128)(2,1)} %param.12) | data formatting | bytes 450560 | tf_op args[1]
  4.1 1.9 %copy.16.stream = bf16[2,110,1024]{2,1,0:T(8,128)(2,1)} copy(bf16[2,110,1024]{2,0,1:T(2,128)(2,1)} %param.11) | data formatting | bytes 901120 | tf_op args[0]
  6.0 1.9 %copy.17.upstream = bf16[2,110,1024]{2,1,0:T(8,128)(2,1)} copy(bf16[2,110,1024]{2,0,1:T(2,128)(2,1)} %param.14) | data formatting | bytes 901120 | tf_op args[3]
  7.9 2.0 %copy.19.sqkv = bf16[2,110,1536]{2,1,0:T(8,128)(2,1)} copy(bf16[2,110,1536]{2,0,1:T(2,128)(2,1)} %param.13) | data formatting | bytes 1351680 | tf_op args[2]
  9.9 116.9 %shard_map.146 = (bf16[2,110,1024]{2,1,0:T(8,128)(2,1)}, bf16[2,110,1536]{2,1,0:T(8,128)(2,1)}, f32[32,384]{1,0:T(8,128)}, f32[32,128]{1,0:T(8,128)}, f32[16,128]{1,0:T(8,128)}) custom-call(bf16[2,110,1024]{2,1,0:T(8,128)(2,1)} %copy.16.stream, bf16[2,110,1024]{2,1,0:T(8,128)(2,1)} %copy.17.upstream, bf16[2,110,512]{2,1,0:T(8,128)(2,1)} %copy.18.so, ...), custom_call_target="tpu_custom_call" | custom-call | tf_op jit(solution)/shard_map/pallas_call | solution.py:696
  126.9 2.2 %copy.20 = bf16[2,110,1024]{2,0,1:T(2,128)(2,1)} copy(bf16[2,110,1024]{2,1,0:T(8,128)(2,1)} %get-tuple-element.21) | data formatting | bytes 901120
  129.1 1.4 %shard_map.147 = (f32[32,384]{1,0:T(8,128)}, f32[32,128]{1,0:T(8,128)}, f32[16,128]{1,0:T(8,128)}) custom-call(f32[32,384]{1,0:T(8,128)} %get-tuple-element.15.q, f32[32,128]{1,0:T(8,128)} %get-tuple-element.16.t, f32[16,128]{1,0:T(8,128)} %get-tuple-element.17.s), custom_call_target="tpu_custom_call" | custom-call | tf_op jit(solution)/shard_map/pallas_call | solution.py:715
  130.6 2.6 %copy.21 = bf16[2,110,1536]{2,0,1:T(2,128)(2,1)} copy(bf16[2,110,1536]{2,1,0:T(8,128)(2,1)} %get-tuple-element.22) | data formatting | bytes 1351680
  (1 shorter events, 0.0 us)
Async XLA Ops:
  0.6 1.1 copy-start

commit v3 on v2

v3 whole, which is shorter than its diff:
```python
import functools

import jax
import jax.numpy as jnp
from jax import lax
from jax.experimental import pallas as pl
from jax.experimental.pallas import tpu as pltpu
from jax.sharding import PartitionSpec as P

MESH = pl.DeviceIdType.MESH
F32 = jnp.float32
BF16 = jnp.bfloat16
D = 1024
E = 64
F = 64
NF = 32
NP = 8
TOK = 110
PAD = 112
SLOT = 4
BUSY = 28
ROWS = F * SLOT
SP = NP * PAD
SCALE = E ** (-0.5)
NEG = -1e30
VLIMIT = 61 * 1024 * 1024


def rcopy(src, dst, ssem, rsem, f, p):
    return pltpu.make_async_remote_copy(
        src_ref=src, dst_ref=dst, send_sem=ssem, recv_sem=rsem, device_id=(f, p), device_id_type=MESH
    )


def swap_halves(a, b):
    axis = a.ndim - 2
    low = lax.broadcasted_iota(jnp.int32, a.shape, axis) < 4
    return jnp.where(low, a, pltpu.roll(b, 4, axis)), jnp.where(low, pltpu.roll(a, 4, axis), b)


def swap_lanes(a, b):
    low = lax.broadcasted_iota(jnp.int32, a.shape, 1) < E
    return jnp.where(low, a, pltpu.roll(b, E, 1)), jnp.where(low, pltpu.roll(a, E, 1), b)


def dot(a, b, da, db):
    return lax.dot_general(a, b, (((da,), (db,)), ((), ())), preferred_element_type=F32)


def place():
    me_f, me_p = lax.axis_index("frame"), lax.axis_index("patch")
    z, y_hi, core = me_f // 4, lax.rem(me_f // 2, 2), lax.rem(me_f, 2)
    x, y_lo = me_p // 2, lax.rem(me_p, 2)
    return z, y_hi, core, x, y_lo


def device(z, y, core, x):
    return z * 4 + (y // 2) * 2 + core, x * 2 + lax.rem(y, 2)


def barrier():
    me_f, me_p = lax.axis_index("frame"), lax.axis_index("patch")
    z, y_hi, core, x, y_lo = place()
    sem = pltpu.get_barrier_semaphore()

    def greet(f, p):
        pl.semaphore_signal(sem, inc=1, device_id=(f, p), device_id_type=MESH)

    def frames(k, _):
        greet(lax.rem(me_f + k, NF), me_p)
        return 0

    lax.fori_loop(1, NF, frames, 0)

    def patches(k, _):
        greet(me_f, lax.rem(me_p + k, NP))
        return 0

    lax.fori_loop(1, NP, patches, 0)

    def across(k, _):
        greet(*device(z, (1 - y_hi) * 2 + lax.rem(k, 2), core, k // 2))
        return 0

    lax.fori_loop(0, NP, across, 0)
    pl.semaphore_wait(sem, NF - 1 + 2 * NP - 1)


class Exchange:
    def __init__(self, src, dst, sems, along_frame, sends=None, takes=None):
        self.src, self.dst, (self.ssem, self.rsem) = src, dst, sems
        self.along_frame, self.sends, self.takes = along_frame, sends, takes
        self.me_f, self.me_p = lax.axis_index("frame"), lax.axis_index("patch")
        self.me = self.me_f if along_frame else self.me_p
        self.n = NF if along_frame else NP

    def copy(self, to, src, dst):
        where = (to, self.me_p) if self.along_frame else (self.me_f, to)
        return rcopy(src, dst, self.ssem.at[0], self.rsem.at[0], *where)

    def start(self):
        def body(k, _):
            to = lax.rem(self.me + k, self.n)

            def go():
                self.copy(to, self.src.at[to], self.dst.at[self.me]).start()

            if self.sends is None:
                go()
            else:
                pl.when(self.sends[0](to))(go)
            return 0

        lax.fori_loop(1, self.n, body, 0)

    def all_of(self, cases, act):
        for condition, count in cases or [(None, self.n - 1)]:

            def go(count=count):
                to = lax.rem(self.me + 1, self.n)
                act(self.copy(to, self.src.at[0:count], self.dst.at[0:count]))

            if condition is None:
                go()
            else:
                pl.when(condition)(go)

    def land(self):
        self.all_of(self.takes, lambda c: c.wait_recv())

    def gone(self):
        self.all_of(self.sends and self.sends[1], lambda c: c.wait_send())


class Sum:
    def __init__(self, term, bufs, x_first):
        self.term, self.x_first = term, x_first
        (self.r0, self.t2, self.t3, self.in1, self.up1, self.full1, self.in2, self.up2, self.full2, self.r3,
         self.ssem, self.rsem) = bufs
        self.z, self.y_hi, self.core, self.x, self.y_lo = place()
        self.y = self.y_hi * 2 + self.y_lo
        self.cols = term.shape[-1]

    def chunk(self, stage, j):
        if stage == 1:
            if self.x_first:
                return self.term.at[:, :, self.core, j]
            return self.term.at[:, j // 2, self.core, :, lax.rem(j, 2)]
        if self.x_first:
            return self.t2.at[:, j // 2, lax.rem(j, 2)]
        return self.t2.at[:, j]

    def ring(self, stage):
        if (stage == 1) == self.x_first:
            return self.x, lambda j: device(self.z, self.y, self.core, j)
        return self.y, lambda j: device(self.z, j, self.core, self.x)

    def core_copy(self, x, y_lo):
        other = 1 - self.core
        s = x * 2 + y_lo
        return rcopy(
            self.term.at[:, :, other, x, y_lo], self.r0.at[:, :, x, y_lo], self.ssem.at[s], self.rsem.at[s],
            *device(self.z, self.y, other, self.x),
        )

    def core_add(self, x, y_lo):
        self.core_copy(x, y_lo).wait_recv()

        def body(z, _):
            mine = self.term[z, :, self.core, x, y_lo].astype(F32)
            self.term[z, :, self.core, x, y_lo] = (mine + self.r0[z, :, x, y_lo].astype(F32)).astype(BF16)
            return 0

        lax.fori_loop(0, 8, body, 0)

    def first(self, stage):
        me, at = self.ring(stage)
        far = lax.rem(me + 2, 4)
        into = self.in1 if stage == 1 else self.in2
        s = 8 if stage == 1 else 12
        return [
            rcopy(
                self.chunk(stage, far).at[4 * h : 4 * h + 4], into.at[h], self.ssem.at[s + h], self.rsem.at[s + h],
                *at(lax.rem(me + (1, 3)[h], 4)),
            )
            for h in range(2)
        ]

    def second(self, stage):
        me, at = self.ring(stage)
        up = self.up1 if stage == 1 else self.up2
        full = self.full1 if stage == 1 else self.full2
        s = 10 if stage == 1 else 14
        return [
            rcopy(up.at[h], full.at[h], self.ssem.at[s + h], self.rsem.at[s + h], *at(lax.rem(me + (1, 3)[h], 4)))
            for h in range(2)
        ]

    def relay(self, stage):
        me, _ = self.ring(stage)
        into = self.in1 if stage == 1 else self.in2
        up = self.up1 if stage == 1 else self.up2
        firsts, seconds = self.first(stage), self.second(stage)
        for h in range(2):
            mine = self.chunk(stage, lax.rem(me + (1, 3)[h], 4))
            firsts[h].wait_recv()

            def body(z, _):
                a = 4 * h + z
                b = 4 * (1 - h) + z
                up[h, a] = (mine[a].astype(F32) + into[h, z].astype(F32)).astype(BF16)
                up[h, b] = mine[b]
                return 0

            lax.fori_loop(0, 4, body, 0)
            seconds[h].start()

    def ring_add(self, stage):
        me, _ = self.ring(stage)
        full = self.full1 if stage == 1 else self.full2
        out = self.t2 if stage == 1 else self.t3
        mine = self.chunk(stage, me)
        for c in self.second(stage):
            c.wait_recv()

        def body(z, _):
            total = mine[z].astype(F32) + full[0, z].astype(F32) + full[1, z].astype(F32)
            out[z] = total.astype(BF16)
            return 0

        lax.fori_loop(0, 8, body, 0)

    def last(self):
        out = []
        for k in range(1, 8):
            to = lax.rem(self.z + k, 8)
            out.append(
                rcopy(
                    self.t3.at[to], self.r3.at[k - 1], self.ssem.at[15 + k], self.rsem.at[15 + k],
                    *device(to, self.y, self.core, self.x),
                )
            )
        return out

    def total(self):
        total = self.t3[self.z].astype(F32)
        for c in self.last():
            c.wait_recv()
        for k in range(7):
            total = total + self.r3[k].astype(F32)
        return total

    def start(self, copies):
        for c in copies:
            c.start()

    def gone(self):
        for x in range(4):
            for y_lo in range(2):
                self.core_copy(x, y_lo).wait_send()
        for c in self.first(1) + self.second(1) + self.first(2) + self.second(2) + self.last():
            c.wait_send()


class PlaneSum(Sum):
    def __init__(self, term, bufs):
        self.term = term
        self.r0, self.t3, self.inp, self.r3, self.ssem, self.rsem, self.psem, self.qsem = bufs
        self.z, self.y_hi, self.core, self.x, self.y_lo = place()
        self.y = self.y_hi * 2 + self.y_lo

    def plane(self, act):
        def body(k, _):
            to = lax.rem(self.x * 4 + self.y + k, 16)
            x, y = to // 4, lax.rem(to, 4)
            act(
                rcopy(
                    self.term.at[:, y // 2, self.core, x, lax.rem(y, 2)], self.inp.at[k - 1],
                    self.psem.at[k - 1], self.qsem.at[k - 1], *device(self.z, y, self.core, x),
                )
            )
            return 0

        lax.fori_loop(1, 16, body, 0)

    def plane_add(self):
        self.plane(lambda c: c.wait_recv())

        def body(z, _):
            total = self.term[z, self.y_hi, self.core, self.x, self.y_lo].astype(F32)
            for k in range(15):
                total = total + self.inp[k, z].astype(F32)
            self.t3[z] = total.astype(BF16)
            return 0

        lax.fori_loop(0, 8, body, 0)

    def gone(self):
        for x in range(4):
            for y_lo in range(2):
                self.core_copy(x, y_lo).wait_send()
        self.plane(lambda c: c.wait_send())
        for c in self.last():
            c.wait_send()


def sum_scratch(cols, x_first):
    mid = (2, 2) if x_first else (4,)
    tile = (16, cols)
    return [
        pltpu.VMEM((8, 2, 4, 2) + tile, BF16),
        pltpu.VMEM((8,) + mid + tile, BF16),
        pltpu.VMEM((8,) + tile, BF16),
        pltpu.VMEM((2, 4) + mid + tile, BF16),
        pltpu.VMEM((2, 8) + mid + tile, BF16),
        pltpu.VMEM((2, 8) + mid + tile, BF16),
        pltpu.VMEM((2, 4) + tile, BF16),
        pltpu.VMEM((2, 8) + tile, BF16),
        pltpu.VMEM((2, 8) + tile, BF16),
        pltpu.VMEM((7,) + tile, BF16),
        pltpu.SemaphoreType.DMA((23,)),
        pltpu.SemaphoreType.DMA((23,)),
    ]


def plane_scratch(cols):
    tile = (16, cols)
    return [
        pltpu.VMEM((8, 2, 4, 2) + tile, BF16),
        pltpu.VMEM((8,) + tile, BF16),
        pltpu.VMEM((15, 8) + tile, BF16),
        pltpu.VMEM((7,) + tile, BF16),
        pltpu.SemaphoreType.DMA((23,)),
        pltpu.SemaphoreType.DMA((23,)),
        pltpu.SemaphoreType.DMA((15,)),
        pltpu.SemaphoreType.DMA((15,)),
    ]


NSUM = 12
TR = 2 * PAD


def whole_kernel(
    stream, upstream, noise, mod, pos, memo, so_hbm, sqkv_hbm, wqkv_hbm, wp_hbm, wps_hbm,
    gs_out, recv_b0, recv_b1, tot_a, tot_b, tot_p,
    so, sqkv, wqkv, wp, wps, wsem,
    xbuf, ubuf, nbuf, gainbuf, send_n, recv_n, send_u, recv_u, ssem, rsem, ssem_u, rsem_u, lsem,
    send_s, recv_s, ssem_s, rsem_s,
    bias, nv, uv, nt, proj, g, o, dqkv, ot, tprobs,
    gn, recv_gn, ssem_n, rsem_n,
    sopad, gosbuf, send_g, recv_g, ssem_g, rsem_g,
    kq, probs, send_b0, ssem_b0, rsem_b0, send_b1, ssem_b1, rsem_b1,
    term_a, term_b, term_p, *sum_bufs,
):
    me_f, me_p = lax.axis_index("frame"), lax.axis_index("patch")
    owner = me_f < BUSY
    loads = [
        pltpu.make_async_copy(src, dst, wsem.at[i])
        for i, (src, dst) in enumerate(
            ((sqkv_hbm, sqkv), (wqkv_hbm, wqkv), (wp_hbm, wp), (wps_hbm, wps), (so_hbm, so))
        )
    ]
    for c in loads:
        c.start()
    sum_a = Sum(term_a, sum_bufs[0:NSUM], True)
    sum_b = Sum(term_b, sum_bufs[NSUM : 2 * NSUM], False)
    sum_p = PlaneSum(term_p, sum_bufs[2 * NSUM :])

    counter = lax.broadcasted_iota(jnp.int32, (1, 128), 1).astype(F32)
    frequency = jnp.exp(-jnp.log(10000.0) * counter / 128)
    waves = []
    for f in range(2):
        angles = noise[f].astype(F32) * frequency
        waves.append(jnp.concatenate([jnp.cos(angles), jnp.sin(angles)], axis=1))
    embedding = jnp.concatenate(waves * 4, axis=0).astype(BF16)
    gainbuf[...] = 1.0 + dot(embedding, mod[...], 1, 0)

    def gain():
        return jnp.broadcast_to(gainbuf[...].reshape(1, 8, D), (TR // 8, 8, D)).reshape(TR, D)

    def inverse_of(x):
        return lax.rsqrt(jnp.mean(x * x, axis=-1, keepdims=True) + 1e-06)

    xbuf[216:TR] = jnp.zeros((8, D), F32)
    ubuf[216:TR] = jnp.zeros((8, D), F32)
    xbuf[0 : 2 * TOK] = stream[...].astype(F32).reshape(2 * TOK, D)
    ubuf[0 : 2 * TOK] = upstream[...].astype(F32).reshape(2 * TOK, D)
    x = xbuf[...]
    nbuf[...] = x * inverse_of(x) * gain()

    def pack(i, _):
        rows = pl.ds(pl.multiple_of(i * 8, 8), 8)
        for buf, to in ((nbuf, send_n), (ubuf, send_u)):
            part = buf[rows]
            to[i] = jnp.concatenate([part[:, 0:512], part[:, 512:1024]], axis=0).astype(BF16)
        return 0

    lax.fori_loop(0, BUSY, pack, 0)

    @pl.when(jnp.logical_not(owner))
    def _():
        recv_n[...] = jnp.zeros(recv_n.shape, BF16)
        recv_u[...] = jnp.zeros(recv_u.shape, BF16)

    barrier()
    to_owners = [(owner, BUSY - 1), (jnp.logical_not(owner), BUSY)]
    from_all = [(owner, NF - 1)]
    out_n = Exchange(send_n, recv_n, (ssem, rsem), True, (lambda d: d < BUSY, to_owners), from_all)
    out_u = Exchange(send_u, recv_u, (ssem_u, rsem_u), True, (lambda d: d < BUSY, to_owners), from_all)
    out_n.start()
    out_l = [
        pltpu.make_async_copy(send_n.at[me_f], recv_n.at[me_f], lsem.at[0]),
        pltpu.make_async_copy(send_u.at[me_f], recv_u.at[me_f], lsem.at[1]),
    ]

    @pl.when(owner)
    def _():
        out_l[0].start()
        out_l[1].start()

    loads[0].wait()
    send_s[:, :, 96:PAD] = jnp.zeros((NP, 3, 16, 128), BF16)
    for j in range(4):
        v = []
        for f in range(2):
            q0 = sqkv[:, f, 128 * j : 128 * j + 128].astype(F32)
            k0 = sqkv[:, f, 512 + 128 * j : 640 + 128 * j].astype(F32)
            m0, m1 = swap_lanes(q0, k0)
            send_s[2 * j, f, 0:TOK] = m0.astype(BF16)
            send_s[2 * j + 1, f, 0:TOK] = m1.astype(BF16)
            v.append(sqkv[:, f, 1024 + 128 * j : 1152 + 128 * j].astype(F32))
        m0, m1 = swap_lanes(v[0], v[1])
        send_s[2 * j, 2, 0:TOK] = m0.astype(BF16)
        send_s[2 * j + 1, 2, 0:TOK] = m1.astype(BF16)
    recv_s[me_p] = send_s[me_p]
    sopad[208:TR] = jnp.zeros((16, 512), BF16)
    loads[4].wait()
    sopad[0 : 2 * TOK] = so[...].astype(F32).reshape(2 * TOK, 512).astype(BF16)

    table = jnp.concatenate(
        [pos[...].astype(F32), memo[...].astype(F32), jnp.zeros((3, F), F32)], axis=0
    ).astype(BF16)
    frame_col = lax.rem(lax.broadcasted_iota(jnp.int32, (F, 128), 1), F)
    at_col = lax.broadcasted_iota(jnp.int32, (F, 128), 0) == frame_col
    at_row = lax.broadcasted_iota(jnp.int32, (F, F), 0) == lax.broadcasted_iota(jnp.int32, (F, F), 1)
    asked = dot(table, jnp.where(at_col, 1.0, 0.0).astype(BF16), 1, 0)
    held = dot(jnp.where(at_row, 1.0, 0.0).astype(BF16), table, 1, 1)
    key_frame = lax.broadcasted_iota(jnp.int32, (F, 128), 0).astype(F32)
    seen = held[:, 0:1] <= asked[0:1]
    for m in range(4):
        seen = jnp.logical_or(seen, key_frame == asked[1 + m : 2 + m])
    bias[...] = jnp.where(seen, 0.0, NEG).astype(F32)

    i = lax.broadcasted_iota(jnp.int32, (ROWS, ROWS), 1)
    wanted = lax.rem(i // 2, SLOT) * F + (i // 8) * 2 + lax.rem(i, 2)
    order = jnp.where(lax.broadcasted_iota(jnp.int32, (ROWS, ROWS), 0) == wanted, 1.0, 0.0).astype(BF16)

    def arrived(ref):
        x = ref[...].astype(F32)
        x = jnp.concatenate([x[:, 0:8], x[:, 8:16]], axis=2).reshape(ROWS, D).astype(BF16)
        return dot(order, x, 1, 0).astype(BF16)

    out_n.gone()
    out_u.start()
    head_x = Exchange(send_s, recv_s, (ssem_s, rsem_s), False)
    head_x.start()

    out_n.land()

    @pl.when(owner)
    def _():
        out_l[0].wait()

    loads[1].wait()

    nv[...] = arrived(recv_n)
    nt[...] = nv[...].T

    def project(c, _):
        cols = pl.ds(pl.multiple_of(c * 512, 512), 512)
        proj[:, cols] = dot(nv[...], wqkv[:, cols], 1, 0).astype(BF16)
        return 0

    lax.fori_loop(0, 6, project, 0)

    low_t = lax.broadcasted_iota(jnp.int32, (F, 128), 1) < E

    def two_heads(x):
        x = x.astype(F32)
        return jnp.concatenate([jnp.where(low_t, x, 0.0), jnp.where(low_t, 0.0, x)], axis=0).astype(BF16)

    def cols_of(j, base):
        return pl.ds(pl.multiple_of(base + j * 128, 128), 128)

    slots = [slice(F * s, F * s + F) for s in range(SLOT)]

    def temporal_probs(j, _):
        made = []
        for rows in slots:
            k = (proj[rows, cols_of(j, D)].astype(F32) * SCALE).astype(BF16)
            st = dot(k, two_heads(proj[rows, cols_of(j, 0)]), 1, 1) + bias[...]
            e = jnp.exp(st - jnp.max(st, axis=0, keepdims=True))
            made.append((e * (1.0 / jnp.sum(e, axis=0, keepdims=True))).astype(BF16))
        for rows, p in zip(slots, made):
            tprobs[j, rows] = p
        return 0

    lax.fori_loop(0, 8, temporal_probs, 0)

    out_u.land()

    @pl.when(owner)
    def _():
        out_l[1].wait()

    loads[2].wait()

    uv[...] = arrived(recv_u)

    def project_g(c, _):
        cols = pl.ds(pl.multiple_of(c * 512, 512), 512)
        g[:, cols] = dot(uv[...], wp[cols, :], 1, 1).astype(BF16)
        return 0

    lax.fori_loop(0, 2, project_g, 0)

    def pair(j, _):
        held = []
        for rows in slots:
            k, v = proj[rows, cols_of(j, D)], proj[rows, cols_of(j, 2 * D)]
            q, gr = two_heads(proj[rows, cols_of(j, 0)]), two_heads(g[rows, cols_of(j, 0)])
            pb = tprobs[j, rows]
            p = pb.astype(F32)
            dp = dot((v.astype(F32) * SCALE).astype(BF16), gr, 1, 1)
            ds = (p * (dp - jnp.sum(p * dp, axis=0, keepdims=True))).astype(BF16)
            held.append((q, k, v, gr, pb, ds))
        made = [
            (dot(pb, v, 0, 0), dot(ds, k, 0, 0), dot(ds, q, 1, 0), dot(pb, gr, 1, 0))
            for q, k, v, gr, pb, ds in held
        ]
        for rows, (out, dq, dk, dv) in zip(slots, made):
            o[rows, cols_of(j, 0)] = jnp.where(low_t, out[0:F], out[F : 2 * F]).astype(BF16)
            dqkv[rows, cols_of(j, 0)] = jnp.where(low_t, dq[0:F], dq[F : 2 * F]).astype(BF16)
            dqkv[rows, cols_of(j, D)] = dk.astype(BF16)
            dqkv[rows, cols_of(j, 2 * D)] = dv.astype(BF16)
        return 0

    lax.fori_loop(0, 8, pair, 0)

    back = dot(order, dot(dqkv[...], wqkv[...], 1, 1).astype(BF16), 0, 0).reshape(NF, 8, D)
    gn[...] = jnp.concatenate([back[:, :, 0:512], back[:, :, 512:1024]], axis=1).astype(BF16)
    back_x = Exchange(gn, recv_gn, (ssem_n, rsem_n), True, (lambda d: owner, from_all), to_owners)
    back_x.start()
    back_l = pltpu.make_async_copy(gn.at[me_f], recv_gn.at[me_f], lsem.at[2])

    @pl.when(owner)
    def _():
        back_l.start()

    ot[...] = o[...].T
    z, y_hi, core, x, y_lo = place()

    def weights(cx, cy):
        p = cx * 2 + cy
        r = dot(nt[...], dqkv[:, pl.ds(pl.multiple_of(p * 384, 128), 384)], 1, 0)
        r = r.reshape(8, 2, 2, 32, 384)
        s = dot(ot[...], uv[:, pl.ds(pl.multiple_of(p * 128, 128), 128)], 1, 0)
        s = s.reshape(8, 2, 2, 32, 128)
        term_a[:, :, :, cx, cy, :, 0:384] = r[:, :, :, 0:16].astype(BF16)
        term_a[:, :, :, cx, cy, :, 384:512] = s[:, :, :, 0:16].astype(BF16)
        sum_a.core_copy(cx, cy).start()
        term_b[:, :, :, cx, cy, :, 0:384] = r[:, :, :, 16:32].astype(BF16)
        term_b[:, :, :, cx, cy, :, 384:512] = s[:, :, :, 16:32].astype(BF16)
        sum_b.core_copy(cx, cy).start()

    def cores(cx, cy):
        sum_a.core_add(cx, cy)
        sum_b.core_add(cx, cy)

    turns = [(2, 0), (2, 1), (1, 0), (3, 0), (0, 0), (1, 1), (3, 1), (0, 1)]
    turns = [(lax.rem(x + dx, 4), lax.rem(y_lo + dy, 2)) for dx, dy in turns]
    for n, turn in enumerate(turns):
        weights(*turn)
        if n >= 2:
            cores(*turns[n - 2])
        if n == 3:
            sum_a.start(sum_a.first(1))
        if n == 6:
            sum_b.start(sum_b.first(1))
    cores(*turns[-2])
    cores(*turns[-1])

    sum_a.relay(1)

    head_x.land()
    low = lax.broadcasted_iota(jnp.int32, (SP, 128), 1) < E
    dead = lax.rem(lax.broadcasted_iota(jnp.int32, (SP, 128), 0), PAD) >= TOK
    dead_bias = jnp.where(dead, NEG, 0.0).astype(F32)
    for f in range(2):
        x = recv_s[:, f].reshape(SP, 128).astype(F32)
        kq[...] = jnp.where(low, pltpu.roll(x, E, 1) * SCALE, 0.0).astype(BF16)
        for b in range(SP // 128):
            rows = slice(b * 128, b * 128 + 128)
            st = dot(kq[...], x[rows].astype(BF16), 1, 1) + dead_bias
            e = jnp.exp(st - jnp.max(st, axis=0, keepdims=True))
            probs[f, :, rows] = (e * (1.0 / jnp.sum(e, axis=0, keepdims=True))).astype(BF16)
    loads[3].wait()

    back_x.land()

    @pl.when(owner)
    def _():
        back_l.wait()

    came = recv_gn[0:BUSY].astype(F32)
    scaled = jnp.concatenate([came[:, 0:8], came[:, 8:16]], axis=2).reshape(TR, D) * gain()
    x = xbuf[...]
    inverse = inverse_of(x)
    inner = jnp.mean(x * scaled, axis=-1, keepdims=True)
    gs = (ubuf[...] + inverse * scaled - x * (inverse * inverse * inverse) * inner).astype(BF16)
    gs_out[...] = gs
    gos = dot(gs, wps[...], 1, 1)
    for j in range(4):
        gosbuf[j] = gos[:, 128 * j : 128 * j + 128]
    for j in range(4):
        m0, m1 = swap_lanes(gosbuf[j, pl.ds(0, PAD, stride=2)], gosbuf[j, pl.ds(1, PAD, stride=2)])
        send_g[2 * j] = m0.astype(BF16)
        send_g[2 * j + 1] = m1.astype(BF16)
    cot_x = Exchange(send_g, recv_g, (ssem_g, rsem_g), False)
    cot_x.start()
    recv_g[me_p] = send_g[me_p]
    tp = dot(sopad[...], gs, 0, 0)
    for p in range(NP):
        term_p[:, :, :, p // 2, p % 2] = tp[:, 128 * p : 128 * p + 128].reshape(8, 2, 2, 16, 128).astype(BF16)
        sum_p.core_copy(p // 2, p % 2).start()

    sum_b.relay(1)

    for p in range(NP):
        sum_p.core_add(p // 2, p % 2)
    sum_p.plane(lambda c: c.start())

    sum_a.ring_add(1)
    sum_a.start(sum_a.first(2))

    cot_x.land()

    g_all = recv_g[...].reshape(SP, 128)
    v_all = recv_s[:, 2].reshape(SP, 128).astype(F32)

    def spatial(f):
        dv = dot(probs[f], g_all, 1, 0)
        qk = recv_s[:, f].reshape(SP, 128)
        kq[...] = jnp.where(low if f == 0 else jnp.logical_not(low), v_all * SCALE, 0.0).astype(BF16)
        for b in range(SP // 128):
            rows = slice(b * 128, b * 128 + 128)
            p = probs[f, :, rows].astype(F32)
            dp = dot(kq[...], g_all[rows], 1, 1)
            ds = p * (dp - jnp.sum(p * dp, axis=0, keepdims=True))
            probs[f, :, rows] = ds.astype(BF16)
        dk = dot(probs[f], qk, 1, 0)
        dq = dot(probs[f], qk, 0, 0)
        return jnp.where(low, dk, dq).astype(BF16).reshape(NP, PAD, 128), dv

    send_b0[...], dv0 = spatial(0)
    token0 = Exchange(send_b0, recv_b0, (ssem_b0, rsem_b0), False)
    token0.start()
    recv_b0[me_p] = send_b0[me_p]

    sum_b.ring_add(1)
    sum_b.start(sum_b.first(2))

    send_b1[:, 0], dv1 = spatial(1)
    send_b1[:, 1] = jnp.where(low, dv0, dv1).astype(BF16).reshape(NP, PAD, 128)

    sum_a.relay(2)
    token1 = Exchange(send_b1, recv_b1, (ssem_b1, rsem_b1), False)
    token1.start()
    recv_b1[me_p] = send_b1[me_p]
    sum_b.relay(2)

    sum_p.plane_add()
    sum_p.start(sum_p.last())

    for s in (sum_a, sum_b):
        s.ring_add(2)
        s.start(s.last())

    token0.land()
    token1.land()
    tot_a[...] = sum_a.total()
    tot_b[...] = sum_b.total()
    tot_p[...] = sum_p.total()

    for e in (out_u, back_x, head_x, cot_x, token0, token1):
        e.gone()
    for s in (sum_a, sum_b, sum_p):
        s.gone()


def finish_kernel(gs, back0, back1, tot_a, tot_b, tot_p, gs_out, out, out_s, out_q, out_t):
    gs_out[...] = gs[0 : 2 * TOK].astype(F32).reshape(TOK, 2, D).astype(BF16)
    for i, total in enumerate((tot_a, tot_b)):
        out_q[16 * i : 16 * i + 16] = total[:, 0:384]
        out_t[16 * i : 16 * i + 16] = total[:, 384:512]
    out_s[...] = tot_p[...]
    for j in range(4):
        c = 128 * j
        for f in range(2):
            part = back0 if f == 0 else back1.at[:, 0]
            k, q = swap_lanes(part[2 * j].astype(F32), part[2 * j + 1].astype(F32))
            out[:, f, c : c + 128] = q[0:TOK].astype(BF16)
            out[:, f, 512 + c : 640 + c] = k[0:TOK].astype(BF16)
        v = swap_lanes(back1[2 * j, 1].astype(F32), back1[2 * j + 1, 1].astype(F32))
        for f in range(2):
            out[:, f, 1024 + c : 1152 + c] = v[f][0:TOK].astype(BF16)


def shards(
    stream,
    spatial_out,
    spatial_qkv,
    upstream,
    proj_spatial,
    qkv_temporal,
    proj_temporal,
    mod_weight,
    noise_steps,
    positions,
    memory,
):
    vmem = pl.BlockSpec(memory_space=pltpu.VMEM)
    smem = pl.BlockSpec(memory_space=pltpu.SMEM)
    hbm = pl.BlockSpec(memory_space=pl.ANY)

    def arr(*shape, dtype=BF16):
        return pltpu.VMEM(shape, dtype)

    def pair_of(n):
        return [pltpu.SemaphoreType.DMA((n,)), pltpu.SemaphoreType.DMA((n,))]

    def shapes(outs):
        return [jax.ShapeDtypeStruct(s, t) for s, t in outs]

    def by_token(tensor):
        return jnp.transpose(tensor, (1, 0, 2))

    scratch = (
        [
            arr(TOK, 2, 512),
            arr(TOK, 2, 1536),
            arr(D, 3 * D),
            arr(D, D),
            arr(512, D),
            pltpu.SemaphoreType.DMA((5,)),
            arr(TR, D, dtype=F32),
            arr(TR, D, dtype=F32),
            arr(TR, D, dtype=F32),
            arr(8, D, dtype=F32),
            arr(NF, 16, 512),
            arr(NF, 16, 512),
            arr(NF, 16, 512),
            arr(NF, 16, 512),
        ]
        + pair_of(1)
        + pair_of(1)
        + [pltpu.SemaphoreType.DMA((3,)), arr(NP, 3, PAD, 128), arr(NP, 3, PAD, 128)]
        + pair_of(1)
        + [
            arr(F, 128, dtype=F32),
            arr(ROWS, D),
            arr(ROWS, D),
            arr(D, ROWS),
            arr(ROWS, 3 * D),
            arr(ROWS, D),
            arr(ROWS, D),
            arr(ROWS, 3 * D),
            arr(D, ROWS),
            arr(8, ROWS, 128),
            arr(NF, 16, 512),
            arr(NF, 16, 512),
        ]
        + pair_of(1)
        + [arr(TR, 512), arr(4, TR, 128, dtype=F32), arr(NP, PAD, 128), arr(NP, PAD, 128)]
        + pair_of(1)
        + [arr(SP, 128), arr(2, SP, SP), arr(NP, PAD, 128)]
        + pair_of(1)
        + [arr(NP, 2, PAD, 128)]
        + pair_of(1)
        + [arr(8, 2, 2, 4, 2, 16, 512), arr(8, 2, 2, 4, 2, 16, 512), arr(8, 2, 2, 4, 2, 16, 128)]
        + sum_scratch(512, True)
        + sum_scratch(512, False)
        + plane_scratch(128)
    )
    made = pl.pallas_call(
        whole_kernel,
        out_shape=shapes(
            [
                ((TR, D), BF16),
                ((NP, PAD, 128), BF16),
                ((NP, 2, PAD, 128), BF16),
                ((16, 512), F32),
                ((16, 512), F32),
                ((16, 128), F32),
            ]
        ),
        in_specs=[vmem] * 2 + [smem] + [vmem] * 3 + [hbm] * 5,
        out_specs=[vmem] * 6,
        scratch_shapes=scratch,
        compiler_params=pltpu.CompilerParams(vmem_limit_bytes=VLIMIT, collective_id=0, has_side_effects=True),
    )(
        by_token(stream),
        by_token(upstream),
        noise_steps,
        mod_weight,
        positions.reshape(1, F),
        memory.T,
        by_token(spatial_out),
        by_token(spatial_qkv),
        qkv_temporal,
        proj_temporal,
        proj_spatial,
    )
    grad_stream, grad_spatial_qkv, grad_s, grad_q, grad_t = pl.pallas_call(
        finish_kernel,
        out_shape=shapes(
            [
                ((TOK, 2, D), BF16),
                ((TOK, 2, 1536), BF16),
                ((16, 128), F32),
                ((32, 384), F32),
                ((32, 128), F32),
            ]
        ),
        in_specs=[vmem] * 6,
        out_specs=[vmem] * 5,
    )(*made)
    return (by_token(grad_stream), by_token(grad_spatial_qkv), grad_s, grad_q, grad_t)


def solution(mesh):
    in_specs = (
        P("frame", "patch", None),
        P("frame", "patch", None),
        P("frame", "patch", None),
        P("frame", "patch", None),
        P(),
        P(),
        P(),
        P(),
        P("frame"),
        P(),
        P(),
    )
    out_specs = (
        P("frame", "patch", None),
        P("frame", "patch", None),
        P("frame", "patch"),
        P("frame", "patch"),
        P("frame", "patch"),
    )
    return jax.shard_map(shards, mesh=mesh, in_specs=in_specs, out_specs=out_specs, check_vma=False)
```

time: 134 us -> 111 us (0.83)
  local copies, waits for them, and re-layouts: 12.5 us -> 0 us
  Pallas kernels: 118 us -> 110 us
    unnamed x8 -> x0, local copies, waits for them, and re-layouts: 12.5 us -> none
    pallas_call x2, Pallas kernels: 118 us -> 110 us  [the longest x1 106 us: shards(): pl.pallas_call(whole_kernel, out_shape=shapes([((TR, D), BF16), ((NP, PAD...]
where the time goes in v3:
time: 111 us
  Pallas kernels  110 us (99%)
    pallas_call x1, Pallas kernels, shards(): pl.pallas_call(whole_kernel, out_shape=shapes([((TR, D), BF16), ((NP, PAD...  106 us
    pallas_call x1, Pallas kernels, shards(): pl.pallas_call(finish_kernel, out_shape=shapes([((TOK, 2, D), BF16), ((TO...  4.13 us

profile of v3, /device:TPU:16, one launch (start us, length us, event | category | flops | bytes accessed | tf_op | source)
XLA Modules:
  0.0 110.6 jit_solution(305069182617160961)
XLA Ops:
  0.6 105.8 %shard_map.146 = (bf16[224,1024]{1,0:T(8,128)(2,1)}, bf16[8,112,128]{2,1,0:T(8,128)(2,1)}, bf16[8,2,112,128]{3,2,1,0:T(8,128)(2,1)}, f32[16,512]{1,0:T(8,128)}, f32[16,512]{1,0:T(8,128)}, /*index=5*/f32[16,128]{1,0:T(8,128)}) custom-call(bf16[110,2,1024]{2,1,0:T(2,128)(2,1)} %bitcast.9, bf16[110,2,1024]{2,1,0:T(2,128)(2,1)} %bitcast.10, s32[2]{0:T(128)} %noise.1, ...), custom_call_target="tpu_custom_call" | custom-call | tf_op jit(solution)/shard_map/pallas_call | solution.py:796
  106.4 4.1 %shard_map.147 = (bf16[110,2,1024]{2,1,0:T(2,128)(2,1)}, bf16[110,2,1536]{2,1,0:T(2,128)(2,1)}, f32[16,128]{1,0:T(8,128)}, f32[32,384]{1,0:T(8,128)}, f32[32,128]{1,0:T(8,128)}) custom-call(bf16[224,1024]{1,0:T(8,128)(2,1)} %get-tuple-element.16.gs, bf16[8,112,128]{2,1,0:T(8,128)(2,1)} %get-tuple-element.17.back0, ...), custom_call_target="tpu_custom_call" | custom-call | tf_op jit(solution)/shard_map/pallas_call | solution.py:825

commit v4 on v3

--- a/solution.py
+++ b/solution.py
@@ -166,18 +166,16 @@
     def core_add(self, x, y_lo):
         self.core_copy(x, y_lo).wait_recv()
 
-        def body(z, _):
-            mine = self.term[z, :, self.core, x, y_lo].astype(F32)
-            self.term[z, :, self.core, x, y_lo] = (mine + self.r0[z, :, x, y_lo].astype(F32)).astype(BF16)
-            return 0
-
-        lax.fori_loop(0, 8, body, 0)
+        for z in range(0, 8, 4):
+            rows = slice(z, z + 4)
+            mine = self.term[rows, :, self.core, x, y_lo].astype(F32)
+            self.term[rows, :, self.core, x, y_lo] = (mine + self.r0[rows, :, x, y_lo].astype(F32)).astype(BF16)
 
     def first(self, stage):
         me, at = self.ring(stage)
         far = lax.rem(me + 2, 4)
         into = self.in1 if stage == 1 else self.in2
-        s = 8 if stage == 1 else 12
+        s = 8 if stage == 1 else 14
         return [
             rcopy(
                 self.chunk(stage, far).at[4 * h : 4 * h + 4], into.at[h], self.ssem.at[s + h], self.rsem.at[s + h],
@@ -186,13 +184,31 @@
             for h in range(2)
         ]
 
+    def plain(self, stage):
+        me, at = self.ring(stage)
+        full = self.full1 if stage == 1 else self.full2
+        s = 10 if stage == 1 else 16
+        out = []
+        for h in range(2):
+            to = lax.rem(me + (1, 3)[h], 4)
+            rows = slice(4 - 4 * h, 8 - 4 * h)
+            out.append(
+                rcopy(
+                    self.chunk(stage, to).at[rows], full.at[h, rows], self.ssem.at[s + h], self.rsem.at[s + h], *at(to)
+                )
+            )
+        return out
+
     def second(self, stage):
         me, at = self.ring(stage)
         up = self.up1 if stage == 1 else self.up2
         full = self.full1 if stage == 1 else self.full2
-        s = 10 if stage == 1 else 14
+        s = 12 if stage == 1 else 18
         return [
-            rcopy(up.at[h], full.at[h], self.ssem.at[s + h], self.rsem.at[s + h], *at(lax.rem(me + (1, 3)[h], 4)))
+            rcopy(
+                up.at[h], full.at[h, 4 * h : 4 * h + 4], self.ssem.at[s + h], self.rsem.at[s + h],
+                *at(lax.rem(me + (1, 3)[h], 4)),
+            )
             for h in range(2)
         ]
 
@@ -204,15 +220,7 @@
         for h in range(2):
             mine = self.chunk(stage, lax.rem(me + (1, 3)[h], 4))
             firsts[h].wait_recv()
-
-            def body(z, _):
-                a = 4 * h + z
-                b = 4 * (1 - h) + z
-                up[h, a] = (mine[a].astype(F32) + into[h, z].astype(F32)).astype(BF16)
-                up[h, b] = mine[b]
-                return 0
-
-            lax.fori_loop(0, 4, body, 0)
+            up[h] = (mine[4 * h : 4 * h + 4].astype(F32) + into[h].astype(F32)).astype(BF16)
             seconds[h].start()
 
     def ring_add(self, stage):
@@ -220,7 +228,7 @@
         full = self.full1 if stage == 1 else self.full2
         out = self.t2 if stage == 1 else self.t3
         mine = self.chunk(stage, me)
-        for c in self.second(stage):
+        for c in self.plain(stage) + self.second(stage):
             c.wait_recv()
 
         def body(z, _):
@@ -236,7 +244,7 @@
             to = lax.rem(self.z + k, 8)
             out.append(
                 rcopy(
-                    self.t3.at[to], self.r3.at[k - 1], self.ssem.at[15 + k], self.rsem.at[15 + k],
+                    self.t3.at[to], self.r3.at[k - 1], self.ssem.at[19 + k], self.rsem.at[19 + k],
                     *device(to, self.y, self.core, self.x),
                 )
             )
@@ -258,16 +266,39 @@
         for x in range(4):
             for y_lo in range(2):
                 self.core_copy(x, y_lo).wait_send()
-        for c in self.first(1) + self.second(1) + self.first(2) + self.second(2) + self.last():
+        for stage in (1, 2):
+            for c in self.first(stage) + self.plain(stage) + self.second(stage):
+                c.wait_send()
+        for c in self.last():
             c.wait_send()
 
 
-class PlaneSum(Sum):
+class SmallSum(Sum):
     def __init__(self, term, bufs):
         self.term = term
-        self.r0, self.t3, self.inp, self.r3, self.ssem, self.rsem, self.psem, self.qsem = bufs
+        self.r0, self.zin, self.t3, self.pin, self.ssem, self.rsem, self.psem, self.qsem = bufs
         self.z, self.y_hi, self.core, self.x, self.y_lo = place()
         self.y = self.y_hi * 2 + self.y_lo
+
+    def along_z(self):
+        out = []
+        for k in range(1, 8):
+            to = lax.rem(self.z + k, 8)
+            out.append(
+                rcopy(
+                    self.term.at[to, :, self.core], self.zin.at[k - 1], self.ssem.at[7 + k], self.rsem.at[7 + k],
+                    *device(to, self.y, self.core, self.x),
+                )
+            )
+        return out
+
+    def z_add(self):
+        total = self.term[self.z, :, self.core].astype(F32)
+        for c in self.along_z():
+            c.wait_recv()
+        for k in range(7):
+            total = total + self.zin[k].astype(F32)
+        self.t3[...] = total.astype(BF16)
 
     def plane(self, act):
         def body(k, _):
@@ -275,7 +306,7 @@
             x, y = to // 4, lax.rem(to, 4)
             act(
                 rcopy(
-                    self.term.at[:, y // 2, self.core, x, lax.rem(y, 2)], self.inp.at[k - 1],
+                    self.t3.at[y // 2, x, lax.rem(y, 2)], self.pin.at[k - 1],
                     self.psem.at[k - 1], self.qsem.at[k - 1], *device(self.z, y, self.core, x),
                 )
             )
@@ -283,25 +314,20 @@
 
         lax.fori_loop(1, 16, body, 0)
 
-    def plane_add(self):
+    def total(self):
+        total = self.t3[self.y_hi, self.x, self.y_lo].astype(F32)
         self.plane(lambda c: c.wait_recv())
-
-        def body(z, _):
-            total = self.term[z, self.y_hi, self.core, self.x, self.y_lo].astype(F32)
-            for k in range(15):
-                total = total + self.inp[k, z].astype(F32)
-            self.t3[z] = total.astype(BF16)
-            return 0
-
-        lax.fori_loop(0, 8, body, 0)
+        for k in range(15):
+            total = total + self.pin[k].astype(F32)
+        return total
 
     def gone(self):
         for x in range(4):
             for y_lo in range(2):
                 self.core_copy(x, y_lo).wait_send()
+        for c in self.along_z():
+            c.wait_send()
         self.plane(lambda c: c.wait_send())
-        for c in self.last():
-            c.wait_send()
 
 
 def sum_scratch(cols, x_first):
@@ -312,38 +338,38 @@
         pltpu.VMEM((8,) + mid + tile, BF16),
         pltpu.VMEM((8,) + tile, BF16),
         pltpu.VMEM((2, 4) + mid + tile, BF16),
-        pltpu.VMEM((2, 8) + mid + tile, BF16),
+        pltpu.VMEM((2, 4) + mid + tile, BF16),
         pltpu.VMEM((2, 8) + mid + tile, BF16),
         pltpu.VMEM((2, 4) + tile, BF16),
-        pltpu.VMEM((2, 8) + tile, BF16),
+        pltpu.VMEM((2, 4) + tile, BF16),
         pltpu.VMEM((2, 8) + tile, BF16),
         pltpu.VMEM((7,) + tile, BF16),
-        pltpu.SemaphoreType.DMA((23,)),
-        pltpu.SemaphoreType.DMA((23,)),
+        pltpu.SemaphoreType.DMA((27,)),
+        pltpu.SemaphoreType.DMA((27,)),
     ]
 
 
-def plane_scratch(cols):
+def small_scratch(cols):
     tile = (16, cols)
     return [
         pltpu.VMEM((8, 2, 4, 2) + tile, BF16),
-        pltpu.VMEM((8,) + tile, BF16),
-        pltpu.VMEM((15, 8) + tile, BF16),
-        pltpu.VMEM((7,) + tile, BF16),
-        pltpu.SemaphoreType.DMA((23,)),
-        pltpu.SemaphoreType.DMA((23,)),
+        pltpu.VMEM((7, 2, 4, 2) + tile, BF16),
+        pltpu.VMEM((2, 4, 2) + tile, BF16),
+        pltpu.VMEM((15,) + tile, BF16),
+        pltpu.SemaphoreType.DMA((15,)),
+        pltpu.SemaphoreType.DMA((15,)),
         pltpu.SemaphoreType.DMA((15,)),
         pltpu.SemaphoreType.DMA((15,)),
     ]
 
 
-NSUM = 12
+NSUM, NSMALL = 12, 8
 TR = 2 * PAD
 
 
 def whole_kernel(
     stream, upstream, noise, mod, pos, memo, so_hbm, sqkv_hbm, wqkv_hbm, wp_hbm, wps_hbm,
-    gs_out, recv_b0, recv_b1, tot_a, tot_b, tot_p,
+    gs_out, recv_b0, recv_b1, tot_a, tot_b, tot_c, tot_p,
     so, sqkv, wqkv, wp, wps, wsem,
     xbuf, ubuf, nbuf, gainbuf, send_n, recv_n, send_u, recv_u, ssem, rsem, ssem_u, rsem_u, lsem,
     send_s, recv_s, ssem_s, rsem_s,
@@ -351,7 +377,7 @@
     gn, recv_gn, ssem_n, rsem_n,
     sopad, gosbuf, send_g, recv_g, ssem_g, rsem_g,
     kq, probs, send_b0, ssem_b0, rsem_b0, send_b1, ssem_b1, rsem_b1,
-    term_a, term_b, term_p, *sum_bufs,
+    term_a, term_b, term_p, term_c, *sum_bufs,
 ):
     me_f, me_p = lax.axis_index("frame"), lax.axis_index("patch")
     owner = me_f < BUSY
@@ -365,7 +391,8 @@
         c.start()
     sum_a = Sum(term_a, sum_bufs[0:NSUM], True)
     sum_b = Sum(term_b, sum_bufs[NSUM : 2 * NSUM], False)
-    sum_p = PlaneSum(term_p, sum_bufs[2 * NSUM :])
+    sum_p = SmallSum(term_p, sum_bufs[2 * NSUM : 2 * NSUM + NSMALL])
+    sum_c = SmallSum(term_c, sum_bufs[2 * NSUM + NSMALL :])
 
     counter = lax.broadcasted_iota(jnp.int32, (1, 128), 1).astype(F32)
     frequency = jnp.exp(-jnp.log(10000.0) * counter / 128)
@@ -561,37 +588,36 @@
     ot[...] = o[...].T
     z, y_hi, core, x, y_lo = place()
 
-    def weights(cx, cy):
-        p = cx * 2 + cy
-        r = dot(nt[...], dqkv[:, pl.ds(pl.multiple_of(p * 384, 128), 384)], 1, 0)
-        r = r.reshape(8, 2, 2, 32, 384)
-        s = dot(ot[...], uv[:, pl.ds(pl.multiple_of(p * 128, 128), 128)], 1, 0)
-        s = s.reshape(8, 2, 2, 32, 128)
-        term_a[:, :, :, cx, cy, :, 0:384] = r[:, :, :, 0:16].astype(BF16)
-        term_a[:, :, :, cx, cy, :, 384:512] = s[:, :, :, 0:16].astype(BF16)
-        sum_a.core_copy(cx, cy).start()
-        term_b[:, :, :, cx, cy, :, 0:384] = r[:, :, :, 16:32].astype(BF16)
-        term_b[:, :, :, cx, cy, :, 384:512] = s[:, :, :, 16:32].astype(BF16)
-        sum_b.core_copy(cx, cy).start()
-
-    def cores(cx, cy):
-        sum_a.core_add(cx, cy)
-        sum_b.core_add(cx, cy)
-
-    turns = [(2, 0), (2, 1), (1, 0), (3, 0), (0, 0), (1, 1), (3, 1), (0, 1)]
-    turns = [(lax.rem(x + dx, 4), lax.rem(y_lo + dy, 2)) for dx, dy in turns]
+    def weights(cx):
+        r = dot(nt[...], dqkv[:, pl.ds(pl.multiple_of(cx * 768, 128), 768)], 1, 0)
+        s = dot(ot[...], uv[:, pl.ds(pl.multiple_of(cx * 256, 128), 256)], 1, 0)
+        for cy in range(2):
+            q = r[:, 384 * cy : 384 * cy + 384].reshape(8, 2, 2, 32, 384)
+            t = s[:, 128 * cy : 128 * cy + 128].reshape(8, 2, 2, 32, 128)
+            term_a[:, :, :, cx, cy, :, 0:384] = q[:, :, :, 0:16].astype(BF16)
+            term_a[:, :, :, cx, cy, :, 384:512] = t[:, :, :, 0:16].astype(BF16)
+            sum_a.core_copy(cx, cy).start()
+            term_b[:, :, :, cx, cy] = q[:, :, :, 16:32].astype(BF16)
+            sum_b.core_copy(cx, cy).start()
+            term_c[:, :, :, cx, cy] = t[:, :, :, 16:32].astype(BF16)
+            sum_c.core_copy(cx, cy).start()
+
+    def cores(cx):
+        for cy in range(2):
+            sum_a.core_add(cx, cy)
+            sum_b.core_add(cx, cy)
+            sum_c.core_add(cx, cy)
+
+    turns = [lax.rem(x + dx, 4) for dx in (2, 1, 3, 0)]
     for n, turn in enumerate(turns):
-        weights(*turn)
-        if n >= 2:
-            cores(*turns[n - 2])
-        if n == 3:
+        weights(turn)
+        if n >= 1:
+            cores(turns[n - 1])
+        if n == 1:
             sum_a.start(sum_a.first(1))
-        if n == 6:
-            sum_b.start(sum_b.first(1))
-    cores(*turns[-2])
-    cores(*turns[-1])
-
-    sum_a.relay(1)
+    cores(turns[-1])
+    sum_a.start(sum_a.plain(1))
+    sum_b.start(sum_b.first(1) + sum_b.plain(1))
 
     head_x.land()
     low = lax.broadcasted_iota(jnp.int32, (SP, 128), 1) < E
@@ -608,6 +634,7 @@
     loads[3].wait()
 
     back_x.land()
+    sum_c.start(sum_c.along_z())
 
     @pl.when(owner)
     def _():
@@ -635,14 +662,12 @@
         term_p[:, :, :, p // 2, p % 2] = tp[:, 128 * p : 128 * p + 128].reshape(8, 2, 2, 16, 128).astype(BF16)
         sum_p.core_copy(p // 2, p % 2).start()
 
+    sum_a.relay(1)
     sum_b.relay(1)
 
     for p in range(NP):
         sum_p.core_add(p // 2, p % 2)
-    sum_p.plane(lambda c: c.start())
-
-    sum_a.ring_add(1)
-    sum_a.start(sum_a.first(2))
+    sum_p.start(sum_p.along_z())
 
     cot_x.land()
 
@@ -668,42 +693,50 @@
     token0.start()
     recv_b0[me_p] = send_b0[me_p]
 
-    sum_b.ring_add(1)
-    sum_b.start(sum_b.first(2))
-
     send_b1[:, 0], dv1 = spatial(1)
     send_b1[:, 1] = jnp.where(low, dv0, dv1).astype(BF16).reshape(NP, PAD, 128)
 
-    sum_a.relay(2)
+    sum_b.ring_add(1)
+    sum_b.start(sum_b.first(2) + sum_b.plain(2))
+
+    sum_a.ring_add(1)
+    sum_a.start(sum_a.first(2) + sum_a.plain(2))
     token1 = Exchange(send_b1, recv_b1, (ssem_b1, rsem_b1), False)
     token1.start()
     recv_b1[me_p] = send_b1[me_p]
+
     sum_b.relay(2)
-
-    sum_p.plane_add()
-    sum_p.start(sum_p.last())
-
-    for s in (sum_a, sum_b):
+    sum_a.relay(2)
+
+    sum_c.z_add()
+    sum_c.plane(lambda c: c.start())
+
+    for s in (sum_b, sum_a):
         s.ring_add(2)
         s.start(s.last())
+
+    sum_p.z_add()
+    sum_p.plane(lambda c: c.start())
 
     token0.land()
     token1.land()
     tot_a[...] = sum_a.total()
     tot_b[...] = sum_b.total()
+    tot_c[...] = sum_c.total()
     tot_p[...] = sum_p.total()
 
     for e in (out_u, back_x, head_x, cot_x, token0, token1):
         e.gone()
-    for s in (sum_a, sum_b, sum_p):
+    for s in (sum_a, sum_b, sum_p, sum_c):
         s.gone()
 
 
-def finish_kernel(gs, back0, back1, tot_a, tot_b, tot_p, gs_out, out, out_s, out_q, out_t):
+def finish_kernel(gs, back0, back1, tot_a, tot_b, tot_c, tot_p, gs_out, out, out_s, out_q, out_t):
     gs_out[...] = gs[0 : 2 * TOK].astype(F32).reshape(TOK, 2, D).astype(BF16)
-    for i, total in enumerate((tot_a, tot_b)):
-        out_q[16 * i : 16 * i + 16] = total[:, 0:384]
-        out_t[16 * i : 16 * i + 16] = total[:, 384:512]
+    out_q[0:16] = tot_a[:, 0:384]
+    out_q[16:32] = tot_b[...]
+    out_t[0:16] = tot_a[:, 384:512]
+    out_t[16:32] = tot_c[...]
     out_s[...] = tot_p[...]
     for j in range(4):
         c = 128 * j
@@ -788,10 +821,12 @@
         + pair_of(1)
         + [arr(NP, 2, PAD, 128)]
         + pair_of(1)
-        + [arr(8, 2, 2, 4, 2, 16, 512), arr(8, 2, 2, 4, 2, 16, 512), arr(8, 2, 2, 4, 2, 16, 128)]
+        + [arr(8, 2, 2, 4, 2, 16, 512), arr(8, 2, 2, 4, 2, 16, 384)]
+        + [arr(8, 2, 2, 4, 2, 16, 128), arr(8, 2, 2, 4, 2, 16, 128)]
         + sum_scratch(512, True)
-        + sum_scratch(512, False)
-        + plane_scratch(128)
+        + sum_scratch(384, False)
+        + small_scratch(128)
+        + small_scratch(128)
     )
     made = pl.pallas_call(
         whole_kernel,
@@ -801,12 +836,13 @@
                 ((NP, PAD, 128), BF16),
                 ((NP, 2, PAD, 128), BF16),
                 ((16, 512), F32),
-                ((16, 512), F32),
+                ((16, 384), F32),
+                ((16, 128), F32),
                 ((16, 128), F32),
             ]
         ),
         in_specs=[vmem] * 2 + [smem] + [vmem] * 3 + [hbm] * 5,
-        out_specs=[vmem] * 6,
+        out_specs=[vmem] * 7,
         scratch_shapes=scratch,
         compiler_params=pltpu.CompilerParams(vmem_limit_bytes=VLIMIT, collective_id=0, has_side_effects=True),
     )(
@@ -833,7 +869,7 @@
                 ((32, 128), F32),
             ]
         ),
-        in_specs=[vmem] * 6,
+        in_specs=[vmem] * 7,
         out_specs=[vmem] * 5,
     )(*made)
     return (by_token(grad_stream), by_token(grad_spatial_qkv), grad_s, grad_q, grad_t)

time: 111 us -> 102 us (0.919)
  Pallas kernels: 110 us -> 101 us
    pallas_call x1, Pallas kernels: 106 us -> 97.1 us  [shards(): pl.pallas_call(whole_kernel, out_shape=shapes([((TR, D), BF16), ((NP, PAD...]
where the time goes in v4:
time: 102 us
  Pallas kernels  101 us (99%)
    pallas_call x1, Pallas kernels, shards(): pl.pallas_call(whole_kernel, out_shape=shapes([((TR, D), BF16), ((NP, PAD...  97.1 us
    pallas_call x1, Pallas kernels, shards(): pl.pallas_call(finish_kernel, out_shape=shapes([((TOK, 2, D), BF16), ((TO...  4.14 us

profile of v4, /device:TPU:16, one launch (start us, length us, event | category | flops | bytes accessed | tf_op | source)
XLA Modules:
  0.0 101.8 jit_solution(1941325824213169519)
XLA Ops:
  0.6 97.1 %shard_map.146 = (bf16[224,1024]{1,0:T(8,128)(2,1)}, bf16[8,112,128]{2,1,0:T(8,128)(2,1)}, bf16[8,2,112,128]{3,2,1,0:T(8,128)(2,1)}, f32[16,512]{1,0:T(8,128)}, ...) custom-call(bf16[110,2,1024]{2,1,0:T(2,128)(2,1)} %bitcast.9, bf16[110,2,1024]{2,1,0:T(2,128)(2,1)} %bitcast.10, ...), custom_call_target="tpu_custom_call" | custom-call | tf_op jit(solution)/shard_map/pallas_call | solution.py:831
  97.7 4.1 %shard_map.147 = (bf16[110,2,1024]{2,1,0:T(2,128)(2,1)}, bf16[110,2,1536]{2,1,0:T(2,128)(2,1)}, f32[16,128]{1,0:T(8,128)}, f32[32,384]{1,0:T(8,128)}, f32[32,128]{1,0:T(8,128)}) custom-call(bf16[224,1024]{1,0:T(8,128)(2,1)} %get-tuple-element.17.gs, bf16[8,112,128]{2,1,0:T(8,128)(2,1)} %get-tuple-element.18.back0, ...), custom_call_target="tpu_custom_call" | custom-call | tf_op jit(solution)/shard_map/pallas_call | solution.py:861

commit v5 on v4

--- a/solution.py
+++ b/solution.py
@@ -330,6 +330,48 @@
         self.plane(lambda c: c.wait_send())
 
 
+class PlaneSum(Sum):
+    def __init__(self, term, bufs):
+        self.term = term
+        self.r0, self.t3, self.inp, self.r3, self.ssem, self.rsem, self.psem, self.qsem = bufs
+        self.z, self.y_hi, self.core, self.x, self.y_lo = place()
+        self.y = self.y_hi * 2 + self.y_lo
+
+    def plane(self, act):
+        def body(k, _):
+            to = lax.rem(self.x * 4 + self.y + k, 16)
+            x, y = to // 4, lax.rem(to, 4)
+            act(
+                rcopy(
+                    self.term.at[:, y // 2, self.core, x, lax.rem(y, 2)], self.inp.at[k - 1],
+                    self.psem.at[k - 1], self.qsem.at[k - 1], *device(self.z, y, self.core, x),
+                )
+            )
+            return 0
+
+        lax.fori_loop(1, 16, body, 0)
+
+    def plane_add(self):
+        self.plane(lambda c: c.wait_recv())
+
+        def body(z, _):
+            total = self.term[z, self.y_hi, self.core, self.x, self.y_lo].astype(F32)
+            for k in range(15):
+                total = total + self.inp[k, z].astype(F32)
+            self.t3[z] = total.astype(BF16)
+            return 0
+
+        lax.fori_loop(0, 8, body, 0)
+
+    def gone(self):
+        for x in range(4):
+            for y_lo in range(2):
+                self.core_copy(x, y_lo).wait_send()
+        self.plane(lambda c: c.wait_send())
+        for c in self.last():
+            c.wait_send()
+
+
 def sum_scratch(cols, x_first):
     mid = (2, 2) if x_first else (4,)
     tile = (16, cols)
@@ -358,6 +400,20 @@
         pltpu.VMEM((15,) + tile, BF16),
         pltpu.SemaphoreType.DMA((15,)),
         pltpu.SemaphoreType.DMA((15,)),
+        pltpu.SemaphoreType.DMA((15,)),
+        pltpu.SemaphoreType.DMA((15,)),
+    ]
+
+
+def plane_scratch(cols):
+    tile = (16, cols)
+    return [
+        pltpu.VMEM((8, 2, 4, 2) + tile, BF16),
+        pltpu.VMEM((8,) + tile, BF16),
+        pltpu.VMEM((15, 8) + tile, BF16),
+        pltpu.VMEM((7,) + tile, BF16),
+        pltpu.SemaphoreType.DMA((27,)),
+        pltpu.SemaphoreType.DMA((27,)),
         pltpu.SemaphoreType.DMA((15,)),
         pltpu.SemaphoreType.DMA((15,)),
     ]
@@ -391,7 +447,7 @@
         c.start()
     sum_a = Sum(term_a, sum_bufs[0:NSUM], True)
     sum_b = Sum(term_b, sum_bufs[NSUM : 2 * NSUM], False)
-    sum_p = SmallSum(term_p, sum_bufs[2 * NSUM : 2 * NSUM + NSMALL])
+    sum_p = PlaneSum(term_p, sum_bufs[2 * NSUM : 2 * NSUM + NSMALL])
     sum_c = SmallSum(term_c, sum_bufs[2 * NSUM + NSMALL :])
 
     counter = lax.broadcasted_iota(jnp.int32, (1, 128), 1).astype(F32)
@@ -667,7 +723,7 @@
 
     for p in range(NP):
         sum_p.core_add(p // 2, p % 2)
-    sum_p.start(sum_p.along_z())
+    sum_p.plane(lambda c: c.start())
 
     cot_x.land()
 
@@ -693,30 +749,29 @@
     token0.start()
     recv_b0[me_p] = send_b0[me_p]
 
+    sum_b.ring_add(1)
+    sum_b.start(sum_b.first(2) + sum_b.plain(2))
+
+    sum_a.ring_add(1)
+    sum_a.start(sum_a.first(2) + sum_a.plain(2))
+
     send_b1[:, 0], dv1 = spatial(1)
     send_b1[:, 1] = jnp.where(low, dv0, dv1).astype(BF16).reshape(NP, PAD, 128)
 
-    sum_b.ring_add(1)
-    sum_b.start(sum_b.first(2) + sum_b.plain(2))
-
-    sum_a.ring_add(1)
-    sum_a.start(sum_a.first(2) + sum_a.plain(2))
+    sum_b.relay(2)
+    sum_a.relay(2)
     token1 = Exchange(send_b1, recv_b1, (ssem_b1, rsem_b1), False)
     token1.start()
     recv_b1[me_p] = send_b1[me_p]
 
-    sum_b.relay(2)
-    sum_a.relay(2)
-
     sum_c.z_add()
     sum_c.plane(lambda c: c.start())
+    sum_p.plane_add()
+    sum_p.start(sum_p.last())
 
     for s in (sum_b, sum_a):
         s.ring_add(2)
         s.start(s.last())
-
-    sum_p.z_add()
-    sum_p.plane(lambda c: c.start())
 
     token0.land()
     token1.land()
@@ -825,7 +880,7 @@
         + [arr(8, 2, 2, 4, 2, 16, 128), arr(8, 2, 2, 4, 2, 16, 128)]
         + sum_scratch(512, True)
         + sum_scratch(384, False)
-        + small_scratch(128)
+        + plane_scratch(128)
         + small_scratch(128)
     )
     made = pl.pallas_call(

time: 102 us -> 104 us (1.020)
  Pallas kernels: 101 us -> 103 us
    pallas_call x1, Pallas kernels: 97.1 us -> 99.1 us  [shards(): pl.pallas_call(whole_kernel, out_shape=shapes([((TR, D), BF16), ((NP, PAD...]
where the time goes in v5:
time: 104 us
  Pallas kernels  103 us (99%)
    pallas_call x1, Pallas kernels, shards(): pl.pallas_call(whole_kernel, out_shape=shapes([((TR, D), BF16), ((NP, PAD...  99.1 us
    pallas_call x1, Pallas kernels, shards(): pl.pallas_call(finish_kernel, out_shape=shapes([((TOK, 2, D), BF16), ((TO...  4.14 us

profile of v5, /device:TPU:16, one launch (start us, length us, event | category | flops | bytes accessed | tf_op | source)
XLA Modules:
  0.0 103.9 jit_solution(13633164147675905718)
XLA Ops:
  0.6 99.1 %shard_map.146 = (bf16[224,1024]{1,0:T(8,128)(2,1)}, bf16[8,112,128]{2,1,0:T(8,128)(2,1)}, bf16[8,2,112,128]{3,2,1,0:T(8,128)(2,1)}, f32[16,512]{1,0:T(8,128)}, ...) custom-call(bf16[110,2,1024]{2,1,0:T(2,128)(2,1)} %bitcast.9, bf16[110,2,1024]{2,1,0:T(2,128)(2,1)} %bitcast.10, ...), custom_call_target="tpu_custom_call" | custom-call | tf_op jit(solution)/shard_map/pallas_call | solution.py:886
  99.7 4.1 %shard_map.147 = (bf16[110,2,1024]{2,1,0:T(2,128)(2,1)}, bf16[110,2,1536]{2,1,0:T(2,128)(2,1)}, f32[16,128]{1,0:T(8,128)}, f32[32,384]{1,0:T(8,128)}, f32[32,128]{1,0:T(8,128)}) custom-call(bf16[224,1024]{1,0:T(8,128)(2,1)} %get-tuple-element.17.gs, bf16[8,112,128]{2,1,0:T(8,128)(2,1)} %get-tuple-element.18.back0, ...), custom_call_target="tpu_custom_call" | custom-call | tf_op jit(solution)/shard_map/pallas_call | solution.py:916

commit v6 on v4

--- a/solution.py
+++ b/solution.py
@@ -363,13 +363,13 @@
     ]
 
 
-NSUM, NSMALL = 12, 8
+NSUM = 12
 TR = 2 * PAD
 
 
 def whole_kernel(
     stream, upstream, noise, mod, pos, memo, so_hbm, sqkv_hbm, wqkv_hbm, wp_hbm, wps_hbm,
-    gs_out, recv_b0, recv_b1, tot_a, tot_b, tot_c, tot_p,
+    gs_out, recv_b0, recv_b1, tot_a, tot_b, tot_p,
     so, sqkv, wqkv, wp, wps, wsem,
     xbuf, ubuf, nbuf, gainbuf, send_n, recv_n, send_u, recv_u, ssem, rsem, ssem_u, rsem_u, lsem,
     send_s, recv_s, ssem_s, rsem_s,
@@ -377,7 +377,7 @@
     gn, recv_gn, ssem_n, rsem_n,
     sopad, gosbuf, send_g, recv_g, ssem_g, rsem_g,
     kq, probs, send_b0, ssem_b0, rsem_b0, send_b1, ssem_b1, rsem_b1,
-    term_a, term_b, term_p, term_c, *sum_bufs,
+    term_a, term_b, term_p, *sum_bufs,
 ):
     me_f, me_p = lax.axis_index("frame"), lax.axis_index("patch")
     owner = me_f < BUSY
@@ -391,8 +391,7 @@
         c.start()
     sum_a = Sum(term_a, sum_bufs[0:NSUM], True)
     sum_b = Sum(term_b, sum_bufs[NSUM : 2 * NSUM], False)
-    sum_p = SmallSum(term_p, sum_bufs[2 * NSUM : 2 * NSUM + NSMALL])
-    sum_c = SmallSum(term_c, sum_bufs[2 * NSUM + NSMALL :])
+    sum_p = SmallSum(term_p, sum_bufs[2 * NSUM :])
 
     counter = lax.broadcasted_iota(jnp.int32, (1, 128), 1).astype(F32)
     frequency = jnp.exp(-jnp.log(10000.0) * counter / 128)
@@ -597,16 +596,14 @@
             term_a[:, :, :, cx, cy, :, 0:384] = q[:, :, :, 0:16].astype(BF16)
             term_a[:, :, :, cx, cy, :, 384:512] = t[:, :, :, 0:16].astype(BF16)
             sum_a.core_copy(cx, cy).start()
-            term_b[:, :, :, cx, cy] = q[:, :, :, 16:32].astype(BF16)
+            term_b[:, :, :, cx, cy, :, 0:384] = q[:, :, :, 16:32].astype(BF16)
+            term_b[:, :, :, cx, cy, :, 384:512] = t[:, :, :, 16:32].astype(BF16)
             sum_b.core_copy(cx, cy).start()
-            term_c[:, :, :, cx, cy] = t[:, :, :, 16:32].astype(BF16)
-            sum_c.core_copy(cx, cy).start()
 
     def cores(cx):
         for cy in range(2):
             sum_a.core_add(cx, cy)
             sum_b.core_add(cx, cy)
-            sum_c.core_add(cx, cy)
 
     turns = [lax.rem(x + dx, 4) for dx in (2, 1, 3, 0)]
     for n, turn in enumerate(turns):
@@ -634,7 +631,6 @@
     loads[3].wait()
 
     back_x.land()
-    sum_c.start(sum_c.along_z())
 
     @pl.when(owner)
     def _():
@@ -701,15 +697,12 @@
 
     sum_a.ring_add(1)
     sum_a.start(sum_a.first(2) + sum_a.plain(2))
+
+    sum_b.relay(2)
+    sum_a.relay(2)
     token1 = Exchange(send_b1, recv_b1, (ssem_b1, rsem_b1), False)
     token1.start()
     recv_b1[me_p] = send_b1[me_p]
-
-    sum_b.relay(2)
-    sum_a.relay(2)
-
-    sum_c.z_add()
-    sum_c.plane(lambda c: c.start())
 
     for s in (sum_b, sum_a):
         s.ring_add(2)
@@ -722,21 +715,20 @@
     token1.land()
     tot_a[...] = sum_a.total()
     tot_b[...] = sum_b.total()
-    tot_c[...] = sum_c.total()
     tot_p[...] = sum_p.total()
 
     for e in (out_u, back_x, head_x, cot_x, token0, token1):
         e.gone()
-    for s in (sum_a, sum_b, sum_p, sum_c):
+    for s in (sum_a, sum_b, sum_p):
         s.gone()
 
 
-def finish_kernel(gs, back0, back1, tot_a, tot_b, tot_c, tot_p, gs_out, out, out_s, out_q, out_t):
+def finish_kernel(gs, back0, back1, tot_a, tot_b, tot_p, gs_out, out, out_s, out_q, out_t):
     gs_out[...] = gs[0 : 2 * TOK].astype(F32).reshape(TOK, 2, D).astype(BF16)
     out_q[0:16] = tot_a[:, 0:384]
-    out_q[16:32] = tot_b[...]
+    out_q[16:32] = tot_b[:, 0:384]
     out_t[0:16] = tot_a[:, 384:512]
-    out_t[16:32] = tot_c[...]
+    out_t[16:32] = tot_b[:, 384:512]
     out_s[...] = tot_p[...]
     for j in range(4):
         c = 128 * j
@@ -821,11 +813,10 @@
         + pair_of(1)
         + [arr(NP, 2, PAD, 128)]
         + pair_of(1)
-        + [arr(8, 2, 2, 4, 2, 16, 512), arr(8, 2, 2, 4, 2, 16, 384)]
-        + [arr(8, 2, 2, 4, 2, 16, 128), arr(8, 2, 2, 4, 2, 16, 128)]
+        + [arr(8, 2, 2, 4, 2, 16, 512), arr(8, 2, 2, 4, 2, 16, 512)]
+        + [arr(8, 2, 2, 4, 2, 16, 128)]
         + sum_scratch(512, True)
-        + sum_scratch(384, False)
-        + small_scratch(128)
+        + sum_scratch(512, False)
         + small_scratch(128)
     )
     made = pl.pallas_call(
@@ -836,13 +827,12 @@
                 ((NP, PAD, 128), BF16),
                 ((NP, 2, PAD, 128), BF16),
                 ((16, 512), F32),
-                ((16, 384), F32),
-                ((16, 128), F32),
+                ((16, 512), F32),
                 ((16, 128), F32),
             ]
         ),
         in_specs=[vmem] * 2 + [smem] + [vmem] * 3 + [hbm] * 5,
-        out_specs=[vmem] * 7,
+        out_specs=[vmem] * 6,
         scratch_shapes=scratch,
         compiler_params=pltpu.CompilerParams(vmem_limit_bytes=VLIMIT, collective_id=0, has_side_effects=True),
     )(
@@ -869,7 +859,7 @@
                 ((32, 128), F32),
             ]
         ),
-        in_specs=[vmem] * 7,
+        in_specs=[vmem] * 6,
         out_specs=[vmem] * 5,
     )(*made)
     return (by_token(grad_stream), by_token(grad_spatial_qkv), grad_s, grad_q, grad_t)

time: 102 us -> 103 us (level)
  no operation moved by 1% of the time
where the time goes in v6:
time: 103 us; the launch traced here: 102 us
  Pallas kernels  102 us (99%)
    pallas_call x1, Pallas kernels, shards(): pl.pallas_call(whole_kernel, out_shape=shapes([((TR, D), BF16), ((NP, PAD...  97.4 us
    pallas_call x1, Pallas kernels, shards(): pl.pallas_call(finish_kernel, out_shape=shapes([((TOK, 2, D), BF16), ((TO...  4.13 us

profile of v6, /device:TPU:16, one launch (start us, length us, event | category | flops | bytes accessed | tf_op | source)
XLA Modules:
  0.0 102.2 jit_solution(17312408159271308417)
XLA Ops:
  0.6 97.4 %shard_map.146 = (bf16[224,1024]{1,0:T(8,128)(2,1)}, bf16[8,112,128]{2,1,0:T(8,128)(2,1)}, bf16[8,2,112,128]{3,2,1,0:T(8,128)(2,1)}, f32[16,512]{1,0:T(8,128)}, f32[16,512]{1,0:T(8,128)}, /*index=5*/f32[16,128]{1,0:T(8,128)}) custom-call(bf16[110,2,1024]{2,1,0:T(2,128)(2,1)} %bitcast.9, bf16[110,2,1024]{2,1,0:T(2,128)(2,1)} %bitcast.10, s32[2]{0:T(128)} %noise.1, ...), custom_call_target="tpu_custom_call" | custom-call | tf_op jit(solution)/shard_map/pallas_call | solution.py:822
  98.1 4.1 %shard_map.147 = (bf16[110,2,1024]{2,1,0:T(2,128)(2,1)}, bf16[110,2,1536]{2,1,0:T(2,128)(2,1)}, f32[16,128]{1,0:T(8,128)}, f32[32,384]{1,0:T(8,128)}, f32[32,128]{1,0:T(8,128)}) custom-call(bf16[224,1024]{1,0:T(8,128)(2,1)} %get-tuple-element.16.gs, bf16[8,112,128]{2,1,0:T(8,128)(2,1)} %get-tuple-element.17.back0, ...), custom_call_target="tpu_custom_call" | custom-call | tf_op jit(solution)/shard_map/pallas_call | solution.py:851
